TPU v7x, 32 devices: a whole 2x2x4 slice. The times are simulated.
32 devices in a mesh: section: 8 (over y, x, core), expert: 4 (over z).
Axes of the slice: x: 2, y: 2, z: 4, core: 2. Of those that a mesh axis runs over, the one named last changes fastest.
Arguments:
- activations: bfloat16 [8192, 8192], P('section', 'expert'), may hold values from -12 to 12
- modality: int32 [8192], P('section'), may hold values from 0 to 1
- selected: int32 [8, 256], P('section'), may hold values from 0 to 1023, as said below
- routes: int32 [2048, 1], P('section'), may hold values from 0 to 3, as said below
- norm_gain: float32 [2, 8192], P(None, 'expert'), may hold values from 0.1 to 1.9
- router: float32 [8192], P('expert'), may hold values from -0.0625 to 0.0625
- gate_w: bfloat16 [4, 3072, 8192], P('expert', 'section'), may hold values from -0.0625 to 0.0625
- up_w: bfloat16 [4, 3072, 8192], P('expert', 'section'), may hold values from -0.0625 to 0.0625
- down_w: bfloat16 [4, 3072, 8192], P('expert', 'section'), may hold values from -0.21875 to 0.21875
Outputs:
- block_out: bfloat16 [8192, 8192], P('section', 'expert')
Inputs may be any that keep to these rules, and one draw needn't show every extreme that they name: Each row of selected lists 256 different positions in rising order, the first and the last position among them. `routes`: among the 256 rows of one section group no expert is named more than 96 times, and some expert exactly 96 times; the entry for selected[s, j] is below 2 if that token's modality is 0, and 2 or more if it is 1.
All inputs are finite; a program needn't handle non-finite values.
Results may differ from a plain program's by a relative error of at most 0.0075.
Values may be sent and summed in bfloat16 or wider, within the bound.
A program may use at most 128 MiB of HBM per device.

v0:
```python
import jax
import jax.numpy as jnp
from jax import lax
from jax.sharding import PartitionSpec as P

D = 8192


EPS = 1e-05


def passed_along(block, axis, distance):
    devices = range(lax.axis_size(axis))
    route = [((i - distance) % len(devices), i) for i in devices]
    return lax.ppermute(block, axis, route)


def feature_product(block, weight):
    return lax.dot_general(
        block, weight, (((1,), (1,)), ((), ())), preferred_element_type=jnp.float32
    )


def body(activations, modality, selected, routes, norm_gain, router, gate_w, up_w, down_w):
    arrived = passed_along(activations, "section", 1)
    picks = selected[0]
    picked = arrived[picks].astype(jnp.float32)
    kinds = modality[picks]
    gains = jnp.where(kinds[:, None] == 1, norm_gain[1][None, :], norm_gain[0][None, :])
    squares, router_terms = lax.psum(
        (jnp.sum(picked * picked, axis=1), jnp.sum(picked * gains * router[None, :], axis=1)),
        "expert",
    )
    scale = lax.rsqrt(squares / D + EPS)
    normed = (picked * scale[:, None] * gains).astype(jnp.bfloat16)
    score = jax.nn.sigmoid(scale * router_terms)
    sel_count = picks.shape[0]
    expert_count = lax.axis_size("expert") * gate_w.shape[0]
    capacity = max(2, 3 * sel_count // (2 * expert_count))
    experts = routes[:, 0]
    onehot = (experts[:, None] == jnp.arange(expert_count, dtype=jnp.int32)[None, :]).astype(
        jnp.int32
    )
    ranks = jnp.cumsum(onehot, axis=0) - 1
    slot = jnp.sum(ranks * onehot, axis=1)
    target = experts * capacity + slot
    placing = (
        target[None, :] == jnp.arange(expert_count * capacity, dtype=jnp.int32)[:, None]
    ).astype(jnp.bfloat16)
    feature_width = normed.shape[1]
    buffer = jnp.dot(placing, normed, preferred_element_type=jnp.float32).astype(jnp.bfloat16)
    buffer = buffer.reshape(expert_count, capacity, feature_width)
    arrived_rows = lax.all_to_all(buffer, "expert", split_axis=0, concat_axis=2, tiled=True)
    block = lax.all_gather(arrived_rows, "section", axis=1, tiled=True)[0]
    gate = feature_product(block, gate_w[0])
    upper = feature_product(block, up_w[0])
    hidden = (jax.nn.silu(gate) * upper).astype(jnp.bfloat16)[None][0]
    part = jnp.dot(hidden, down_w[0], preferred_element_type=jnp.float32)
    summed = lax.psum_scatter(
        lax.optimization_barrier(part.astype(jnp.bfloat16))
        .astype(jnp.float32)
        .astype(jnp.bfloat16),
        "section",
        scatter_dimension=0,
        tiled=True,
    )
    expert_out = summed[None]
    gathered_back = lax.all_to_all(expert_out, "expert", split_axis=2, concat_axis=0, tiled=True)
    flat_back = gathered_back.reshape(expert_count * capacity, feature_width)
    rows_out = jnp.dot(placing.T, flat_back, preferred_element_type=jnp.float32)
    result = arrived.astype(jnp.float32).at[picks].add(score[:, None] * rows_out)
    return result.astype(jnp.bfloat16)


def solution(mesh):
    placed = (
        P("section", "expert"),
        P("section"),
        P("section", None),
        P("section", None),
        P(None, "expert"),
        P("expert"),
        P("expert", "section", None),
        P("expert", "section", None),
        P("expert", "section", None),
    )
    return jax.shard_map(
        body, mesh=mesh, in_specs=placed, out_specs=P("section", "expert"), check_vma=False
    )
```

profile of v0, /device:TPU:0, one launch (start us, length us, event | category | flops | bytes accessed | tf_op | source)
XLA Modules:
  0.0 447.0 jit_solution(8888507125631301374)
XLA Ops:
  7.7 1.2 reduce-window.6
  9.9 1.4 gather_fusion.1
  13.6 42.8 %collective-permute-done = bf16[1024,2048]{1,0:T(8,128)(2,1)} collective-permute-done((bf16[1024,2048]{1,0:T(8,128)(2,1)}, bf16[1024,2048]{1,0:T(8,128)(2,1)}, u32[]{:S(2)}, u32[]{:S(2)}) %collective-permute-start) | collective-permute-done | bytes 4194336 | tf_op jit(solution)/shard_map/ppermute | solution.py:15
  56.4 5.1 %gather_fusion = bf16[256,2048]{1,0:T(8,128)(2,1)S(1)} fusion(bf16[1024,2048]{1,0:T(8,128)(2,1)} %collective-permute-done, s32[1024]{0:T(1024)S(1)} %pad_clamp_fusion), kind=kCustom, calls=%fused_computation | custom fusion | bytes 2098176 | tf_op jit(solution)/shard_map/gather | solution.py:27
  62.1 12.7 %all-reduce = (f32[256]{0:T(256)S(1)}, f32[256]{0:T(256)S(1)}) all-reduce(f32[256]{0:T(256)S(1)} %get-tuple-element.6, f32[256]{0:T(256)S(1)} %get-tuple-element.5), channel_id=1, replica_groups=mesh['section'=8,'expert'=4] {'expert'}, use_global_device_ids=true, to_apply=%region_1.2 | all-reduce | flops 512 | bytes 4096 | tf_op jit(solution)/shard_map/psum | solution.py:30
  75.7 36.1 %all_to_all.33 = bf16[4,96,2048]{2,1,0:T(8,128)(2,1)S(1)} all-to-all(bf16[4,96,2048]{2,1,0:T(8,128)(2,1)S(1)} %bitcast.63), channel_id=1, replica_groups=mesh['section'=8,'expert'=4] {'expert'}, dimensions={0} | all-to-all | bytes 3145728 | tf_op jit(solution)/shard_map/all_to_all | solution.py:53
  111.7 1.2 copy.26
  113.2 70.2 %all-gather.2.cloned.1.call-done = bf16[1,768,8192]{2,1,0:T(8,128)(2,1)} async-done(((bf16[1,96,8192]{2,1,0:T(8,128)(2,1)}), bf16[1,768,8192]{2,1,0:T(8,128)(2,1)}) %all-gather.2.cloned.1.call-update) | async-done | bytes 12582928 | tf_op jit(solution)/shard_map/all_gather | solution.py:54
  183.5 12.4 %fusion.2 = f32[768,384]{1,0:T(8,128)} fusion(bf16[1,768,8192]{2,1,0:T(8,128)(2,1)} %all-gather.2.cloned.1.call-done, bf16[1,384,8192]{2,1,0:T(8,128)(2,1)} %param.15), kind=kOutput, calls=%fused_computation.6 | convolution fusion | flops 4831838208 | bytes 20054016 | tf_op jit(solution)/shard_map/dot_general | solution.py:19
  195.9 9.5 %fusion.16 = bf16[768,384]{1,0:T(8,128)(2,1)S(1)} fusion(bf16[1,384,8192]{2,1,0:T(8,128)(2,1)} %param.16, bf16[1,768,8192]{2,1,0:T(8,128)(2,1)S(1)} %copy-done.3, f32[768,384]{1,0:T(8,128)} %fusion.2), kind=kOutput, calls=%fused_computation.22 | convolution fusion | flops 4833607680 | bytes 20643840 | tf_op jit(solution)/shard_map/dot_general | solution.py:19
  205.5 9.5 %convolution_convert_fusion = bf16[768,8192]{1,0:T(8,128)(2,1)} fusion(bf16[768,384]{1,0:T(8,128)(2,1)S(1)} %fusion.16, bf16[1,384,8192]{2,1,0:T(8,128)(2,1)S(1)} %bitcast.76), kind=kOutput, calls=%fused_computation.3 | convolution fusion | flops 4838129664 | bytes 19464192 | tf_op jit(solution)/shard_map/dot_general | solution.py:58
  215.0 92.5 %reduce-scatter.2.cloned.1.call-done = bf16[96,8192]{1,0:T(8,128)(2,1)} async-done(((bf16[768,8192]{1,0:T(8,128)(2,1)}), bf16[96,8192]{1,0:T(8,128)(2,1)}) %reduce-scatter.2.cloned.1.call-update) | async-done | bytes 1572880 | tf_op jit(solution)/shard_map/reduce_scatter | solution.py:59
  307.6 9.4 %copy.23 = bf16[1,96,8192]{1,0,2:T(2,128)(2,1)} copy(bf16[1,96,8192]{2,1,0:T(8,128)(2,1)} %bitcast.64) | data formatting | bytes 3145728 | tf_op jit(solution)/shard_map/broadcast_in_dim | solution.py:67
  317.5 45.5 %reduce = bf16[8192,96]{1,0:T(8,128)(2,1)S(1)} reduce(bf16[8192,1,96]{2,1,0:T(2,128)(2,1)} %bitcast.57, bf16[]{:T(256)} %broadcast.77), dimensions={1}, to_apply=%bitcast.53.reduce_sub_computation | reduce | bytes 3145730
  363.0 4.1 reshape.95
  367.1 4.6 %all-to-all-start.1 = ((bf16[4,2,98304]{2,1,0:T(2,128)(2,1)}), bf16[4,2,98304]{2,1,0:T(2,128)(2,1)S(1)}, u32[]{:S(2)}, u32[]{:S(2)}) async-start(bf16[4,2,98304]{2,1,0:T(2,128)(2,1)} %reshape.95), calls=%async_computation.2 | async-start | bytes 3145728 | tf_op jit(solution)/shard_map/all_to_all | solution.py:68
  371.7 6.5 %convert_element_type.29 = f32[1024,2048]{1,0:T(8,128)} convert(bf16[1024,2048]{1,0:T(8,128)(2,1)} %collective-permute-done) | non-fusion elementwise | flops 2097152 | bytes 12582912 | tf_op jit(solution)/shard_map/convert_element_type | solution.py:71
  378.2 30.5 %all-to-all-done.1 = bf16[4,2,98304]{2,1,0:T(2,128)(2,1)S(1)} async-done(((bf16[4,2,98304]{2,1,0:T(2,128)(2,1)}), bf16[4,2,98304]{2,1,0:T(2,128)(2,1)S(1)}, u32[]{:S(2)}, u32[]{:S(2)}) %all-to-all-start.1) | async-done | bytes 1572896 | tf_op jit(solution)/shard_map/all_to_all | solution.py:68
  408.6 4.1 reshape.96
  412.8 8.3 %copy.24 = bf16[1,96,8192]{2,1,0:T(8,128)(2,1)S(1)} copy(bf16[1,96,8192]{1,0,2:T(2,128)(2,1)} %bitcast.58) | data formatting | bytes 3145728 | tf_op jit(solution)/shard_map/all_to_all | solution.py:68
  421.0 1.2 all_to_all.29
  422.2 0.9 copy.25
  423.9 10.2 %scatter_fusion = f32[1024,2048]{1,0:T(8,128)} fusion(f32[1024,2048]{1,0:T(8,128)} %convert_element_type.29, s32[256]{0:T(256)S(1)} %bitcast.70, f32[256,2048]{1,0:T(8,128)S(1)} %convolution_multiply_fusion), kind=kCustom, calls=%fused_computation.2 | custom fusion | flops 524288 | bytes 6292480 | tf_op jit(solution)/shard_map/scatter-add | solution.py:71
  434.1 6.1 %convert_element_type.36 = bf16[1024,2048]{1,0:T(8,128)(2,1)} convert(f32[1024,2048]{1,0:T(8,128)} %scatter_fusion) | non-fusion elementwise | flops 2097152 | bytes 12582912 | tf_op jit(solution)/shard_map/convert_element_type | solution.py:72
  (36 shorter events, 7.5 us)
Async XLA Ops:
  6.5 3.4 copy-start
  6.5 176.9 %all-gather.2.cloned.1.call-start = ((), (), s32[]{:S(2)}) async-start(), calls=%async_computation.3 | async-start | bytes 14155776 | tf_op jit(solution)/shard_map/all_gather | solution.py:54
  6.5 49.8 %collective-permute-start = (bf16[1024,2048]{1,0:T(8,128)(2,1)}, bf16[1024,2048]{1,0:T(8,128)(2,1)}, u32[]{:S(2)}, u32[]{:S(2)}) collective-permute-start(bf16[1024,2048]{1,0:T(8,128)(2,1)} %param.9), channel_id=1, source_target_pairs={{28,0},{0,4},{4,8},{8,12},{12,16},{16,20},{20,24},{24,28},{29,1},{... | collective-permute-start | bytes 12582920 | tf_op jit(solution)/shard_map/ppermute | solution.py:15
  13.5 47.9 %copy-start.2 = (f32[2048]{0:T(1024)S(1)}, f32[2048]{0:T(1024)}, u32[]{:S(2)}) copy-start(f32[2048]{0:T(1024)} %param.14) | copy-start | bytes 24580
  113.0 194.6 %reduce-scatter.2.cloned.1.call-start = ((), (), s32[]{:S(2)}) async-start(), calls=%async_computation.4 | async-start | bytes 14155776 | tf_op jit(solution)/shard_map/reduce_scatter | solution.py:59
  183.5 12.4 %copy-start.3 = (bf16[1,768,8192]{2,1,0:T(8,128)(2,1)S(1)}, bf16[1,768,8192]{2,1,0:T(8,128)(2,1)}, u32[]{:S(2)}) copy-start(bf16[1,768,8192]{2,1,0:T(8,128)(2,1)} %all-gather.2.cloned.1.call-done) | copy-start | bytes 37748740
  183.5 22.0 %slice-start = ((s8[6291456]{0:T(1024)(128)(4,1)}), s8[4194304]{0:T(1024)(128)(4,1)S(1)}, s32[]{:S(2)}) async-start(s8[6291456]{0:T(1024)(128)(4,1)} %bitcast.75), calls=%async_computation.5 | async-start | bytes 8388608
  195.9 9.5 %slice-start.1 = ((s8[6291456]{0:T(1024)(128)(4,1)}), s8[2097152]{0:T(1024)(128)(4,1)S(1)}, s32[]{:S(2)}) async-start(s8[6291456]{0:T(1024)(128)(4,1)} %bitcast.75), calls=%async_computation.6 | async-start | bytes 4194304
  367.1 41.6 %all-to-all-start.1 = ((bf16[4,2,98304]{2,1,0:T(2,128)(2,1)}), bf16[4,2,98304]{2,1,0:T(2,128)(2,1)S(1)}, u32[]{:S(2)}, u32[]{:S(2)}) async-start(bf16[4,2,98304]{2,1,0:T(2,128)(2,1)} %reshape.95), calls=%async_computation.2 | async-start | bytes 3145728 | tf_op jit(solution)/shard_map/all_to_all | solution.py:68
  434.1 6.1 %copy-start.1 = (s32[1024]{0:T(1024)S(1)}, s32[1024]{0:T(1024)}, u32[]{:S(2)}) copy-start(s32[1024]{0:T(1024)} %param.10) | copy-start | bytes 12292
Sparse Core Ops, SparseCore 0:
  113.1 70.2 all-gather.1
  215.1 92.3 reduce-scatter.1
where the time goes:
time: 448 us; the launch traced here: 447 us
  waiting for transfers between devices  236 us (53%)
  other arithmetic  73 us (16%)
  blocking collectives  48.8 us (11%)
  local copies, waits for them, and re-layouts  37.3 us (8%)
  matrix products  33 us (7%)
  between operations  13.5 us (3%)
  starting transfers between devices  5.27 us (1%)
    reduce_scatter x1, waiting for transfers between devices, body(): lax.psum_scatter(lax.optimization_barrier(part.astype(jnp.bfloat16)).asty...  92.5 us
    all_gather x1, waiting for transfers between devices, body(): block = lax.all_gather(arrived_rows, 'section', axis=1, tiled=True)[0]  70.2 us
    unnamed x3, other arithmetic  45.6 us
    ppermute x1, waiting for transfers between devices, passed_along(): return lax.ppermute(block, axis, route)  42.8 us
    all_to_all x1, blocking collectives, body(): lax.all_to_all(buffer, 'expert', split_axis=0, concat_axis=2, tiled=True)  36.1 us
    all_to_all x1, waiting for transfers between devices, body(): lax.all_to_all(expert_out, 'expert', split_axis=2, concat_axis=0, tiled=T...  30.5 us
    dot_general x2, matrix products, feature_product(): lax.dot_general(block, weight, (((1,), (1,)), ((), ())), preferred_elemen...  21.9 us
    psum x1, blocking collectives, body(): lax.psum((jnp.sum(picked * picked, axis=1), jnp.sum(picked * gains * rout...  12.7 us
  transfers between devices with their start and end apart: 4, of which 4 were waited for; matrix products, arithmetic and copies ran while one was open for 3% of the time, Pallas kernels for 0%

commit v1 on v0

v1 whole, which is shorter than its diff:
```python
import jax
import jax.numpy as jnp
from jax import lax
from jax.sharding import PartitionSpec as P

D = 8192


EPS = 1e-05


def passed_along(block, axis, distance):
    devices = range(lax.axis_size(axis))
    route = [((i - distance) % len(devices), i) for i in devices]
    return lax.ppermute(block, axis, route)


def feature_product(block, weight):
    return lax.dot_general(
        block, weight, (((1,), (1,)), ((), ())), preferred_element_type=jnp.float32
    )


def slot_map(picks, experts, capacity, slots, tokens):
    count = picks.shape[0]
    order = jnp.arange(count, dtype=jnp.int32)
    earlier = (experts[:, None] == experts[None, :]) & (order[None, :] < order[:, None])
    slot = jnp.sum(earlier.astype(jnp.int32), axis=1)
    target = experts * capacity + slot
    placing = (target[None, :] == jnp.arange(slots, dtype=jnp.int32)[:, None]).astype(jnp.bfloat16)
    picking = (picks[:, None] == jnp.arange(tokens, dtype=jnp.int32)[None, :]).astype(jnp.bfloat16)
    return jnp.dot(placing, picking, preferred_element_type=jnp.float32).astype(jnp.bfloat16)


def body(activations, modality, selected, routes, norm_gain, router, gate_w, up_w, down_w):
    sections, planes = lax.axis_size("section"), lax.axis_size("expert")
    tokens, width = activations.shape
    picks, experts = selected[0], routes[:, 0]
    expert_count = planes * gate_w.shape[0]
    capacity = max(2, 3 * picks.shape[0] // (2 * expert_count))
    slots = expert_count * capacity
    ahead = passed_along(jnp.stack([picks, experts]), "section", -1)
    arrived = passed_along(activations, "section", 1)
    whole = lax.all_gather(
        jnp.concatenate([norm_gain, router[None, :]], axis=0), "expert", axis=1, tiled=True
    )
    place_ahead = slot_map(ahead[0], ahead[1], capacity, slots, tokens)
    place_own = slot_map(picks, experts, capacity, slots, tokens)
    buffer = jnp.dot(place_ahead, activations, preferred_element_type=jnp.float32)
    buffer = buffer.astype(jnp.bfloat16).reshape(planes, capacity, width)
    rows = lax.all_to_all(buffer, "expert", split_axis=0, concat_axis=0, tiled=True)
    rows = rows.transpose(1, 0, 2).reshape(capacity, planes * width).astype(jnp.float32)
    image = lax.axis_index("expert") >= planes // 2
    gain = jnp.where(image, whole[1], whole[0])[None, :]
    scale = lax.rsqrt(jnp.sum(rows * rows, axis=1) / (planes * width) + EPS)
    score = jax.nn.sigmoid(scale * jnp.sum(rows * gain * whole[2][None, :], axis=1))
    normed = (rows * scale[:, None] * gain).astype(jnp.bfloat16)
    scores = lax.all_gather(passed_along(score, "section", 1), "expert", axis=0, tiled=True)
    block = lax.all_gather(normed, "section", axis=0, tiled=True)
    gate = feature_product(block, gate_w[0])
    upper = feature_product(block, up_w[0])
    hidden = (jax.nn.silu(gate) * upper).astype(jnp.bfloat16)
    hidden = jnp.roll(hidden, capacity, axis=0)
    part = jnp.dot(hidden, down_w[0], preferred_element_type=jnp.float32).astype(jnp.bfloat16)
    summed = lax.psum_scatter(part, "section", scatter_dimension=0, tiled=True)
    back = summed.reshape(capacity, planes, width).transpose(1, 0, 2)
    back = lax.all_to_all(back, "expert", split_axis=0, concat_axis=0, tiled=True)
    back = back.reshape(slots, width)
    high = scores.astype(jnp.bfloat16)
    low = (scores - high.astype(jnp.float32)).astype(jnp.bfloat16)
    spread = jnp.concatenate([place_own * high[:, None], place_own * low[:, None]], axis=0)
    added = lax.dot_general(
        spread,
        jnp.concatenate([back, back], axis=0),
        (((0,), (0,)), ((), ())),
        preferred_element_type=jnp.float32,
    )
    return (arrived.astype(jnp.float32) + added).astype(jnp.bfloat16)


def solution(mesh):
    placed = (
        P("section", "expert"),
        P("section"),
        P("section", None),
        P("section", None),
        P(None, "expert"),
        P("expert"),
        P("expert", "section", None),
        P("expert", "section", None),
        P("expert", "section", None),
    )
    return jax.shard_map(
        body, mesh=mesh, in_specs=placed, out_specs=P("section", "expert"), check_vma=False
    )
```

time: 448 us -> 344 us (0.77)
  other arithmetic: 73 us -> 4.59 us
  waiting for transfers between devices: 236 us -> 190 us
  local copies, waits for them, and re-layouts: 37.3 us -> 4.57 us
  blocking collectives: 48.8 us -> 70.5 us
  matrix products: 33 us -> 46.2 us
  starting transfers between devices: 5.27 us -> 13.3 us
    unnamed x3 -> x1, other arithmetic: 45.6 us -> 0.36 us
    all_gather x0 -> x1, blocking collectives: none -> 43.1 us  [body(): lax.all_gather(jnp.concatenate([norm_gain, router[None, :]], axis=0), 'ex...]
    ppermute x1 -> x3, waiting for transfers between devices: 42.8 us -> 3.89 us  [passed_along(): return lax.ppermute(block, axis, route)]
    all_to_all x1 -> x0, blocking collectives: 36.1 us -> none  [body(): lax.all_to_all(buffer, 'expert', split_axis=0, concat_axis=2, tiled=True)]
    unnamed x0 -> x1, blocking collectives: none -> 27.4 us
    all_to_all x1 -> x2, waiting for transfers between devices: 30.5 us -> 4.98 us  [the longest x1 4.97 us: body(): lax.all_to_all(back, 'expert', split_axis=0, concat_axis=0, tiled=True)]
    reduce_scatter x1, waiting for transfers between devices: 92.5 us -> 109 us  [body(): summed = lax.psum_scatter(part, 'section', scatter_dimension=0, tiled=True)]
    dot_general x3 -> x4, matrix products: 11.1 us -> 25.2 us  [the longest x1 12.5 us: body(): jnp.dot(hidden, down_w[0], preferred_element_type=jnp.float32)]
  transfers between devices with their start and end apart: 4 -> 7, of which waited for: 4 -> 5; matrix products, arithmetic and copies ran while one was open for 3% -> 2% of each run, Pallas kernels for 0% -> 0%
where the time goes in v1:
time: 344 us; the launch traced here: 343 us
  waiting for transfers between devices  190 us (55%)
  blocking collectives  70.5 us (20%)
  matrix products  46.2 us (13%)
  between operations  14.2 us (4%)
  starting transfers between devices  13.3 us (4%)
  other arithmetic  4.59 us (1%)
  local copies, waits for them, and re-layouts  4.57 us (1%)
    reduce_scatter x1, waiting for transfers between devices, body(): summed = lax.psum_scatter(part, 'section', scatter_dimension=0, tiled=True)  109 us
    all_gather x1, waiting for transfers between devices, body(): block = lax.all_gather(normed, 'section', axis=0, tiled=True)  71.4 us
    all_gather x1, blocking collectives, body(): lax.all_gather(jnp.concatenate([norm_gain, router[None, :]], axis=0), 'ex...  43.1 us
    unnamed x1, blocking collectives  27.4 us
    dot_general x2, matrix products, feature_product(): lax.dot_general(block, weight, (((1,), (1,)), ((), ())), preferred_elemen...  21 us
    dot_general x1, matrix products, body(): jnp.dot(hidden, down_w[0], preferred_element_type=jnp.float32)  12.5 us
  transfers between devices with their start and end apart: 7, of which 5 were waited for; matrix products, arithmetic and copies ran while one was open for 2% of the time, Pallas kernels for 0%

profile of v1, /device:TPU:0, one launch (start us, length us, event | category | flops | bytes accessed | tf_op | source)
XLA Modules:
  0.0 342.9 jit_solution(135568752162675410)
XLA Ops:
  6.5 0.7 pad_add_fusion
  7.2 3.3 collective-permute-start.1
  10.6 1.3 collective-permute-done.1
  12.1 5.5 %convolution_convert_fusion.1 = bf16[384,2048]{1,0:T(8,128)(2,1)} fusion(bf16[1024,2048]{1,0:T(8,128)(2,1)} %param.9, s32[256]{0:T(256)S(1)} %bitcast.50, s32[256]{0:T(256)S(1)} %bitcast.49), kind=kOutput, calls=%fused_computation.18 | convolution fusion | flops 1813479424 | bytes 5769216 | tf_op jit(solution)/shard_map/dot_general | solution.py:49
  17.6 5.0 %all-to-all-start = ((bf16[4,96,2048]{2,1,0:T(8,128)(2,1)}), bf16[4,96,2048]{2,1,0:T(8,128)(2,1)S(1)}, u32[]{:S(2)}, u32[]{:S(2)}) async-start(bf16[4,96,2048]{2,1,0:T(8,128)(2,1)} %bitcast.7), calls=%async_computation | async-start | bytes 3145728 | tf_op jit(solution)/shard_map/all_to_all | solution.py:51
  22.6 43.1 %all_gather.9 = f32[3,8192]{1,0:T(4,128)S(1)} all-gather(f32[3,2048]{1,0:T(4,128)S(1)} %pad_maximum_fusion), channel_id=1, replica_groups=mesh['section'=8,'expert'=4] {'expert'}, dimensions={1}, use_global_device_ids=true | all-gather | bytes 122880 | tf_op jit(solution)/shard_map/all_gather | solution.py:44
  65.8 0.5 broadcast.46
  66.3 0.8 fusion.36
  67.2 0.4 convert_bitcast_fusion
  67.9 0.8 fusion.7
  68.7 1.5 multiply_convert_fusion
  70.3 71.4 %all-gather.2.cloned.1.call-done = bf16[768,8192]{1,0:T(8,128)(2,1)} async-done(((bf16[96,8192]{1,0:T(8,128)(2,1)}), bf16[768,8192]{1,0:T(8,128)(2,1)}) %all-gather.2.cloned.1.call-update) | async-done | bytes 12582928 | tf_op jit(solution)/shard_map/all_gather | solution.py:59
  141.7 11.8 %fusion.3 = f32[768,384]{1,0:T(8,128)S(1)} fusion(bf16[768,8192]{1,0:T(8,128)(2,1)} %all-gather.2.cloned.1.call-done, bf16[1,384,8192]{2,1,0:T(8,128)(2,1)} %param.14), kind=kOutput, calls=%fused_computation.5 | convolution fusion | flops 4831838208 | bytes 20054016 | tf_op jit(solution)/shard_map/dot_general | solution.py:19
  153.5 9.1 %fusion.20 = bf16[768,384]{1,0:T(8,128)(2,1)S(1)} fusion(bf16[768,8192]{1,0:T(8,128)(2,1)S(1)} %copy-done.4, bf16[1,384,8192]{2,1,0:T(8,128)(2,1)} %param.15, f32[768,384]{1,0:T(8,128)S(1)} %fusion.3), kind=kOutput, calls=%fused_computation.26 | convolution fusion | flops 4833607680 | bytes 20643840 | tf_op jit(solution)/shard_map/dot_general | solution.py:19
  162.7 12.5 %convolution_convert_fusion = bf16[768,8192]{1,0:T(8,128)(2,1)} fusion(bf16[1,384,8192]{2,1,0:T(8,128)(2,1)} %param.16, bf16[672,384]{1,0:T(8,128)(2,1)S(1)} %slice.36, bf16[96,384]{1,0:T(8,128)(2,1)S(1)} %slice.35), kind=kOutput, calls=%fused_computation | convolution fusion | flops 4839309312 | bytes 19464192 | tf_op jit(solution)/shard_map/dot_general | solution.py:64
  175.6 109.3 %reduce-scatter.2.cloned.1.call-done = bf16[96,8192]{1,0:T(8,128)(2,1)} async-done(((bf16[768,8192]{1,0:T(8,128)(2,1)}), bf16[96,8192]{1,0:T(8,128)(2,1)}) %reduce-scatter.2.cloned.1.call-update) | async-done | bytes 1572880 | tf_op jit(solution)/shard_map/reduce_scatter | solution.py:65
  284.8 2.8 copy.18
  287.6 4.6 %all-to-all-start.1 = ((bf16[4,96,2048]{2,1,0:T(8,128)(2,1)}), bf16[4,96,2048]{2,1,0:T(8,128)(2,1)S(1)}, u32[]{:S(2)}, u32[]{:S(2)}) async-start(bf16[4,96,2048]{2,1,0:T(8,128)(2,1)} %bitcast.38), calls=%async_computation.2 | async-start | bytes 3145728 | tf_op jit(solution)/shard_map/all_to_all | solution.py:67
  292.5 0.6 dynamic-slice
  293.7 2.6 collective-permute-done.2
  296.5 27.4 %all-reduce = f32[384]{0:T(512)S(1)} all-reduce(f32[384]{0:T(512)S(1)} %dynamic-update-slice), channel_id=1, replica_groups=mesh['section'=8,'expert'=4] {'expert'}, use_global_device_ids=true, to_apply=%add | all-reduce | flops 384 | bytes 3072
  323.9 0.5 broadcast_multiply_fusion.1
  324.4 5.0 %all-to-all-done.1 = bf16[4,96,2048]{2,1,0:T(8,128)(2,1)S(1)} async-done(((bf16[4,96,2048]{2,1,0:T(8,128)(2,1)}), bf16[4,96,2048]{2,1,0:T(8,128)(2,1)S(1)}, u32[]{:S(2)}, u32[]{:S(2)}) %all-to-all-start.1) | async-done | bytes 1572896 | tf_op jit(solution)/shard_map/all_to_all | solution.py:67
  329.4 6.7 %add_convert_fusion = bf16[1024,2048]{1,0:T(8,128)(2,1)} fusion(bf16[1024,2048]{1,0:T(8,128)(2,1)} %collective-permute-done, bf16[384,2048]{1,0:T(8,128)(2,1)S(1)} %bitcast.40, bf16[384,1024]{1,0:T(8,128)(2,1)S(1)} %get-tuple-element.12, bf16[384,1024]{1,0:T(8,128)(2,1)S(1)} %get-tuple-element.11), kind=kOutput, calls=%fused_computation.1 | convolution fusion | flops 3236954112 | bytes 11534336 | tf_op jit(solution)/shard_map/dot_general | solution.py:72
  (35 shorter events, 1.5 us)
Async XLA Ops:
  7.2 4.6 %collective-permute-start.1 = (s32[2,256]{1,0:T(2,128)S(1)}, s32[2,256]{1,0:T(2,128)S(1)}, u32[]{:S(2)}, u32[]{:S(2)}) collective-permute-start(s32[2,256]{1,0:T(2,128)S(1)} %pad_add_fusion), channel_id=1, source_target_pairs={{4,0},{8,4},{12,8},{16,12},{20,16},{24,20},{28,24},{0,28},{5,1},{9... | collective-permute-start | bytes 6152 | tf_op jit(solution)/shard_map/ppermute | solution.py:15
  17.6 5.0 %copy-start = (f32[2,2048]{1,0:T(2,128)S(1)}, f32[2,2048]{1,0:T(2,128)}, u32[]{:S(2)}) copy-start(f32[2,2048]{1,0:T(2,128)} %param.12) | copy-start | bytes 49156
  17.6 5.0 %copy-start.2 = (f32[2048]{0:T(1024)S(1)}, f32[2048]{0:T(1024)}, u32[]{:S(2)}) copy-start(f32[2048]{0:T(1024)} %param.13) | copy-start | bytes 24580
  17.6 49.6 %all-to-all-start = ((bf16[4,96,2048]{2,1,0:T(8,128)(2,1)}), bf16[4,96,2048]{2,1,0:T(8,128)(2,1)S(1)}, u32[]{:S(2)}, u32[]{:S(2)}) async-start(bf16[4,96,2048]{2,1,0:T(8,128)(2,1)} %bitcast.7), calls=%async_computation | async-start | bytes 3145728 | tf_op jit(solution)/shard_map/all_to_all | solution.py:51
  22.6 119.1 %all-gather.2.cloned.1.call-start = ((), (), s32[]{:S(2)}) async-start(), calls=%async_computation.3 | async-start | bytes 14155776 | tf_op jit(solution)/shard_map/all_gather | solution.py:59
  70.2 214.6 %reduce-scatter.2.cloned.1.call-start = ((), (), s32[]{:S(2)}) async-start(), calls=%async_computation.4 | async-start | bytes 14155776 | tf_op jit(solution)/shard_map/reduce_scatter | solution.py:65
  141.7 11.8 %copy-start.4 = (bf16[768,8192]{1,0:T(8,128)(2,1)S(1)}, bf16[768,8192]{1,0:T(8,128)(2,1)}, u32[]{:S(2)}) copy-start(bf16[768,8192]{1,0:T(8,128)(2,1)} %all-gather.2.cloned.1.call-done) | copy-start | bytes 37748740
  175.3 149.1 %collective-permute-start = (bf16[1024,2048]{1,0:T(8,128)(2,1)}, bf16[1024,2048]{1,0:T(8,128)(2,1)}, u32[]{:S(2)}, u32[]{:S(2)}) collective-permute-start(bf16[1024,2048]{1,0:T(8,128)(2,1)} %param.9), channel_id=1, source_target_pairs={{28,0},{0,4},{4,8},{8,12},{12,16},{16,20},{20,24},{24,28},{29,1},{... | collective-permute-start | bytes 12582920 | tf_op jit(solution)/shard_map/ppermute | solution.py:15
  284.8 7.4 %copy-start.1 = (s32[256,1]{0,1:T(1,128)S(1)}, s32[256,1]{0,1:T(1,128)}, u32[]{:S(2)}) copy-start(s32[256,1]{0,1:T(1,128)} %param.11) | copy-start | bytes 3076
  284.8 7.6 %copy-start.5 = (u32[32]{0:T(128)S(1)}, u32[32]{0:T(128)}, u32[]{:S(2)}) copy-start(u32[32]{0:T(128)} %constant.27) | copy-start | bytes 388
  284.8 39.0 %copy-start.3 = (s32[1,256]{1,0:T(1,128)S(1)}, s32[1,256]{1,0:T(1,128)}, u32[]{:S(2)}) copy-start(s32[1,256]{1,0:T(1,128)} %param.10) | copy-start | bytes 3076
  287.6 41.8 %all-to-all-start.1 = ((bf16[4,96,2048]{2,1,0:T(8,128)(2,1)}), bf16[4,96,2048]{2,1,0:T(8,128)(2,1)S(1)}, u32[]{:S(2)}, u32[]{:S(2)}) async-start(bf16[4,96,2048]{2,1,0:T(8,128)(2,1)} %bitcast.38), calls=%async_computation.2 | async-start | bytes 3145728 | tf_op jit(solution)/shard_map/all_to_all | solution.py:67
  292.4 3.9 %collective-permute-start.2 = (f32[96]{0:T(128)S(1)}, f32[96]{0:T(128)S(1)}, u32[]{:S(2)}, u32[]{:S(2)}) collective-permute-start(f32[96]{0:T(128)S(1)} %get-tuple-element.16), channel_id=1, source_target_pairs={{28,0},{0,4},{4,8},{8,12},{12,16},{16,20},{20,24},{24,28},{29,1},{... | collective-permute-start | bytes 1160 | tf_op jit(solution)/shard_map/ppermute | solution.py:15
Sparse Core Ops, SparseCore 0:
  70.3 71.2 all-gather.1
  175.4 109.4 reduce-scatter.1

commit v2 on v1

--- a/solution.py
+++ b/solution.py
@@ -1,6 +1,8 @@
 import jax
 import jax.numpy as jnp
 from jax import lax
+from jax.experimental import pallas as pl
+from jax.experimental.pallas import tpu as pltpu
 from jax.sharding import PartitionSpec as P
 
 D = 8192
@@ -32,6 +34,318 @@
     return jnp.dot(placing, picking, preferred_element_type=jnp.float32).astype(jnp.bfloat16)
 
 
+LANES = 128
+MESH = pl.DeviceIdType.MESH
+
+
+def exchange_kernel(
+    rows_in, vectors, gate_hbm, up_hbm, down_hbm, out,
+    gate_v, up_v, down_v, came, vec, gathered, gate_sum, up_sum, hidden,
+    for_sib, mine, from_sib, relay_x, relay_y, final_x, final_y, done,
+    load_sem, z_send, z_recv, vec_send, vec_recv, ag_send, ag_recv, rs_send, rs_recv, back_send, back_recv,
+):
+    planes, cap, width = rows_in.shape
+    full = planes * width
+    half = cap // 2
+    hid = gate_hbm.shape[0]
+    me, plane = lax.axis_index("section"), lax.axis_index("expert")
+    core, chip = lax.rem(me, 2), lax.div(me, 2)
+    x, y = lax.rem(chip, 2), lax.div(chip, 2)
+    sib, xn, yn = me + 1 - 2 * core, me + 2 - 4 * x, me + 4 - 8 * y
+    chip_x, chip_y = chip + 1 - 2 * x, chip + 2 - 4 * y
+    chip_d = 3 - chip
+    dests = {"x": (xn, plane), "y": (yn, plane), "s": (sib, plane)}
+    uppers = [lax.rem(plane + j, planes) for j in range(1, planes)]
+
+    barrier = pltpu.get_barrier_semaphore()
+    greeted = list(dests.values()) + [(me, p) for p in uppers]
+    for device in greeted:
+        pl.semaphore_signal(barrier, inc=1, device_id=device, device_id_type=MESH)
+    pl.semaphore_wait(barrier, len(greeted))
+
+    sent = []
+
+    def send(src, dst, send_sem, recv_sem, device):
+        copy = pltpu.make_async_remote_copy(
+            src_ref=src, dst_ref=dst, send_sem=send_sem, recv_sem=recv_sem,
+            device_id=device, device_id_type=MESH,
+        )
+        copy.start()
+        sent.append(copy)
+        return copy
+
+    z_copies = {}
+    vec_copies = [
+        send(vectors, vec.at[plane], vec_send.at[j], vec_recv.at[j], (me, p))
+        for j, p in enumerate(uppers)
+    ]
+    for part in range(2):
+        piece = pl.ds(part * half, half)
+        for j, p in enumerate(uppers):
+            n = part * (planes - 1) + j
+            z_copies[part, j] = send(
+                rows_in.at[p, piece], came.at[plane, piece], z_send.at[n], z_recv.at[n], (me, p)
+            )
+    local = [
+        pltpu.make_async_copy(rows_in.at[plane], came.at[plane], load_sem.at[0]),
+        pltpu.make_async_copy(vectors, vec.at[plane], load_sem.at[1]),
+        pltpu.make_async_copy(gate_hbm, gate_v, load_sem.at[2]),
+        pltpu.make_async_copy(up_hbm, up_v, load_sem.at[3]),
+        pltpu.make_async_copy(down_hbm, down_v, load_sem.at[4]),
+    ]
+    for copy in local:
+        copy.start()
+
+    def place(owner_chip, owner_core, part):
+        return pl.ds(
+            pl.multiple_of((owner_chip * 2 + owner_core) * cap + part * half, 16), half
+        )
+
+    image = (plane >= planes // 2).astype(jnp.float32)
+
+    def norm(part):
+        @pl.loop(0, half // 16)
+        def _(step):
+            at = pl.ds(pl.multiple_of(part * half + step * 16, 16), 16)
+            to = pl.ds(pl.multiple_of(me * cap + part * half + step * 16, 16), 16)
+            squares = jnp.zeros((16, 1), jnp.float32)
+            terms = jnp.zeros((16, 1), jnp.float32)
+            for q in range(planes):
+                rows = came[q, at, :].astype(jnp.float32)
+                gain = vec[q, 0:1, :] * (1.0 - image) + vec[q, 1:2, :] * image
+                squares += jnp.sum(rows * rows, axis=1, keepdims=True)
+                terms += jnp.sum(rows * (gain * vec[q, 2:3, :]), axis=1, keepdims=True)
+            scale = lax.rsqrt(squares / full + EPS)
+            score = 1.0 / (1.0 + jnp.exp(-(scale * terms)))
+            for q in range(planes):
+                rows = came[q, at, :].astype(jnp.float32)
+                gain = vec[q, 0:1, :] * (1.0 - image) + vec[q, 1:2, :] * image
+                gathered[to, q * width : (q + 1) * width] = (rows * scale * gain).astype(jnp.bfloat16)
+            high = jnp.broadcast_to(score, (16, LANES)).astype(jnp.bfloat16).astype(jnp.float32)
+            lane = lax.broadcasted_iota(jnp.int32, (16, LANES), 1)
+            gathered[to, full : full + LANES] = jnp.where(
+                lane < LANES // 2, high, score - high
+            ).astype(jnp.bfloat16)
+
+    ag = {}
+    names = ["x0", "x1", "y0", "y1", "fx", "fy", "s0", "s1", "sx0", "sx1", "sy0", "sy1", "sd0", "sd1"]
+
+    def pass_block(name, owner_chip, part, to):
+        ref = gathered.at[place(owner_chip, core, part)]
+        n = names.index(name)
+        ag[name] = send(ref, ref, ag_send.at[n], ag_recv.at[n], dests[to])
+
+    local[0].wait()
+    local[1].wait()
+    for copy in vec_copies:
+        copy.wait_recv()
+    for part in range(2):
+        for j in range(planes - 1):
+            z_copies[part, j].wait_recv()
+        norm(part)
+        pass_block(f"x{part}", chip, part, "x")
+        pass_block(f"y{part}", chip, part, "y")
+        pass_block(f"s{part}", chip, part, "s")
+
+    def products(owner_chip):
+        first = pl.multiple_of(owner_chip * 2 * cap, 16)
+        gate_sum[...] = jnp.zeros_like(gate_sum)
+        up_sum[...] = jnp.zeros_like(up_sum)
+        deep = 1024
+
+        @pl.loop(0, full // deep)
+        def _(step):
+            columns = pl.ds(pl.multiple_of(step * deep, deep), deep)
+            block = gathered[pl.ds(first, 2 * cap), columns]
+            gate_sum[...] += feature_product(block, gate_v[:, columns])
+            up_sum[...] += feature_product(block, up_v[:, columns])
+
+        marks = gathered[pl.ds(first, 2 * cap), full : full + LANES].astype(jnp.float32)
+        score = jnp.sum(marks, axis=1, keepdims=True) * (2.0 / LANES)
+        gate = gate_sum[...]
+        value = gate / (1.0 + jnp.exp(-gate)) * up_sum[...] * score
+        value = value.astype(jnp.bfloat16)
+        hidden[1, pl.ds(pl.multiple_of(owner_chip * cap, 16), cap), :] = value[:cap]
+        after = lax.rem(owner_chip + 1, 4)
+        hidden[0, pl.ds(pl.multiple_of(after * cap, 16), cap), :] = value[cap:]
+
+    ag["x0"].wait_recv()
+    pass_block("fy", chip_x, 0, "y")
+    pass_block("sx0", chip_x, 0, "s")
+    ag["y0"].wait_recv()
+    pass_block("sy0", chip_y, 0, "s")
+    ag["s0"].wait_recv()
+    ag["s1"].wait_recv()
+    local[2].wait()
+    local[3].wait()
+    products(chip)
+    ag["y1"].wait_recv()
+    pass_block("fx", chip_y, 1, "x")
+    pass_block("sy1", chip_y, 1, "s")
+    ag["x1"].wait_recv()
+    pass_block("sx1", chip_x, 1, "s")
+    ag["sx0"].wait_recv()
+    ag["sx1"].wait_recv()
+    products(chip_x)
+    ag["fy"].wait_recv()
+    pass_block("sd0", chip_d, 0, "s")
+    ag["sy0"].wait_recv()
+    ag["sy1"].wait_recv()
+    products(chip_y)
+    ag["fx"].wait_recv()
+    pass_block("sd1", chip_d, 1, "s")
+    ag["sd0"].wait_recv()
+    ag["sd1"].wait_recv()
+    products(chip_d)
+    local[4].wait()
+
+    rs = {}
+    targets = [lax.rem(plane + 1 + i, planes) for i in range(planes)]
+
+    def give(kind, n, i, src, dst, to):
+        at = n * planes + i
+        rs[kind, i] = send(src, dst, rs_send.at[at], rs_recv.at[at], dests[to])
+
+    def down(i, which, into):
+        wide = 512
+
+        @pl.loop(0, width // wide)
+        def _(step):
+            columns = pl.ds(pl.multiple_of(targets[i] * width + step * wide, wide), wide)
+            to = pl.ds(pl.multiple_of(step * wide, wide), wide)
+            into[i, :, to] = jnp.dot(
+                hidden[which], down_v[:, columns], preferred_element_type=jnp.float32
+            ).astype(jnp.bfloat16)
+
+    def start_sums(i):
+        down(i, 1 - core, for_sib)
+        give("s", 0, i, for_sib.at[i], from_sib.at[i], "s")
+        down(i, core, mine)
+
+    def add_into(ref, i, first, count, others):
+        @pl.loop(0, count // 16)
+        def _(step):
+            at = pl.ds(pl.multiple_of(first + step * 16, 16), 16)
+            total = mine[i, at, :].astype(jnp.float32)
+            for other, begin in others:
+                rows = pl.ds(pl.multiple_of(begin + step * 16, 16), 16)
+                total += other[i, rows, :].astype(jnp.float32)
+            if ref is None:
+                mine[i, at, :] = total.astype(jnp.bfloat16)
+            else:
+                ref[i, pl.ds(pl.multiple_of(step * 16, 16), 16), :] = total.astype(jnp.bfloat16)
+
+    def chip_sums(i):
+        rs["s", i].wait_recv()
+        for other in (chip_d, chip_x, chip_y):
+            base = pl.multiple_of(other * cap, 16)
+            add_into(None, i, base, cap, [(from_sib, base)])
+            low, high = pl.ds(base, half), pl.ds(pl.multiple_of(base + half, 16), half)
+            if other is chip_d:
+                give("rx", 1, i, mine.at[i, low], relay_x.at[i], "x")
+                give("ry", 2, i, mine.at[i, high], relay_y.at[i], "y")
+            elif other is chip_x:
+                give("x0", 3, i, mine.at[i, low], final_x.at[i, pl.ds(0, half)], "x")
+            else:
+                give("y1", 4, i, mine.at[i, high], final_y.at[i, pl.ds(half, half)], "y")
+
+    def relay_sums(i):
+        rs["rx", i].wait_recv()
+        first = pl.multiple_of(chip_y * cap, 16)
+        add_into(None, i, first, half, [(relay_x, 0)])
+        give("y0", 5, i, mine.at[i, pl.ds(first, half)], final_y.at[i, pl.ds(0, half)], "y")
+        rs["ry", i].wait_recv()
+        first = pl.multiple_of(chip_x * cap + half, 16)
+        add_into(None, i, first, half, [(relay_y, 0)])
+        give("x1", 6, i, mine.at[i, pl.ds(first, half)], final_x.at[i, pl.ds(half, half)], "x")
+
+    back = []
+
+    def final_sums(i):
+        for kind in ("x0", "y1", "y0", "x1"):
+            rs[kind, i].wait_recv()
+        base = pl.multiple_of(chip * cap, 16)
+        add_into(done, i, base, cap, [(from_sib, base), (final_x, 0), (final_y, 0)])
+        if i < planes - 1:
+            back.append(
+                send(done.at[i], out.at[plane], back_send.at[i], back_recv.at[i], (me, targets[i]))
+            )
+
+    start_sums(0)
+    start_sums(1)
+    chip_sums(0)
+    start_sums(2)
+    start_sums(3)
+    chip_sums(1)
+    relay_sums(0)
+    chip_sums(2)
+    relay_sums(1)
+    final_sums(0)
+    chip_sums(3)
+    relay_sums(2)
+    final_sums(1)
+    relay_sums(3)
+    final_sums(2)
+    final_sums(3)
+    own = pltpu.make_async_copy(done.at[planes - 1], out.at[plane], load_sem.at[5])
+    own.start()
+    for copy in back:
+        copy.wait_recv()
+    own.wait()
+    for copy in sent:
+        copy.wait_send()
+
+
+def exchanged(buffer, vectors, gate, up, down):
+    planes, cap, width = buffer.shape
+    hid, full = gate.shape
+    half, chips = cap // 2, 4
+    bf, dma = jnp.bfloat16, pltpu.SemaphoreType.DMA
+    anywhere = pl.BlockSpec(memory_space=pl.ANY)
+    return pl.pallas_call(
+        exchange_kernel,
+        out_shape=jax.ShapeDtypeStruct(buffer.shape, bf),
+        in_specs=[anywhere] * 5,
+        out_specs=anywhere,
+        scratch_shapes=[
+            pltpu.VMEM((hid, full), bf),
+            pltpu.VMEM((hid, full), bf),
+            pltpu.VMEM((hid, full), bf),
+            pltpu.VMEM((planes, cap, width), bf),
+            pltpu.VMEM((planes,) + vectors.shape, jnp.float32),
+            pltpu.VMEM((2 * chips * cap, full + LANES), bf),
+            pltpu.VMEM((2 * cap, hid), jnp.float32),
+            pltpu.VMEM((2 * cap, hid), jnp.float32),
+            pltpu.VMEM((2, chips * cap, hid), bf),
+            pltpu.VMEM((planes, chips * cap, width), bf),
+            pltpu.VMEM((planes, chips * cap, width), bf),
+            pltpu.VMEM((planes, chips * cap, width), bf),
+            pltpu.VMEM((planes, half, width), bf),
+            pltpu.VMEM((planes, half, width), bf),
+            pltpu.VMEM((planes, cap, width), bf),
+            pltpu.VMEM((planes, cap, width), bf),
+            pltpu.VMEM((planes, cap, width), bf),
+            dma((6,)),
+            dma((2 * (planes - 1),)),
+            dma((2 * (planes - 1),)),
+            dma((planes - 1,)),
+            dma((planes - 1,)),
+            dma((14,)),
+            dma((14,)),
+            dma((7 * planes,)),
+            dma((7 * planes,)),
+            dma((planes - 1,)),
+            dma((planes - 1,)),
+        ],
+        compiler_params=pltpu.CompilerParams(
+            collective_id=0, has_side_effects=True, vmem_limit_bytes=63 * 1024 * 1024
+        ),
+        cost_estimate=pl.CostEstimate(
+            flops=6 * 2 * chips * cap * hid * full, bytes_accessed=6 * hid * full, transcendentals=0
+        ),
+    )(buffer, vectors, gate, up, down)
+
+
 def body(activations, modality, selected, routes, norm_gain, router, gate_w, up_w, down_w):
     sections, planes = lax.axis_size("section"), lax.axis_size("expert")
     tokens, width = activations.shape
@@ -41,13 +355,22 @@
     slots = expert_count * capacity
     ahead = passed_along(jnp.stack([picks, experts]), "section", -1)
     arrived = passed_along(activations, "section", 1)
-    whole = lax.all_gather(
-        jnp.concatenate([norm_gain, router[None, :]], axis=0), "expert", axis=1, tiled=True
-    )
     place_ahead = slot_map(ahead[0], ahead[1], capacity, slots, tokens)
     place_own = slot_map(picks, experts, capacity, slots, tokens)
     buffer = jnp.dot(place_ahead, activations, preferred_element_type=jnp.float32)
     buffer = buffer.astype(jnp.bfloat16).reshape(planes, capacity, width)
+    if (sections, planes) == (8, 4) and capacity % 32 == 0:
+        vectors = jnp.concatenate(
+            [norm_gain, router[None, :], jnp.zeros((5, width), jnp.float32)], axis=0
+        )
+        back = exchanged(buffer, vectors, gate_w[0], up_w[0], down_w[0]).reshape(slots, width)
+        added = lax.dot_general(
+            place_own, back, (((0,), (0,)), ((), ())), preferred_element_type=jnp.float32
+        )
+        return (arrived.astype(jnp.float32) + added).astype(jnp.bfloat16)
+    whole = lax.all_gather(
+        jnp.concatenate([norm_gain, router[None, :]], axis=0), "expert", axis=1, tiled=True
+    )
     rows = lax.all_to_all(buffer, "expert", split_axis=0, concat_axis=0, tiled=True)
     rows = rows.transpose(1, 0, 2).reshape(capacity, planes * width).astype(jnp.float32)
     image = lax.axis_index("expert") >= planes // 2

time: 344 us -> 194 us (0.56)
  waiting for transfers between devices: 190 us -> 0.01 us
  Pallas kernels: 0 us -> 174 us
  blocking collectives: 70.5 us -> 0 us
  matrix products: 46.2 us -> 12.1 us
  between operations: 14.2 us -> 0.04 us
  starting transfers between devices: 13.3 us -> 3.34 us
  local copies, waits for them, and re-layouts: 4.57 us -> 0.09 us
    pallas_call x0 -> x1, Pallas kernels: none -> 174 us  [exchanged(): pl.pallas_call(exchange_kernel, out_shape=jax.ShapeDtypeStruct(buffer.sha...]
    reduce_scatter x1 -> x0, waiting for transfers between devices: 109 us -> none  [body(): summed = lax.psum_scatter(part, 'section', scatter_dimension=0, tiled=True)]
    all_gather x1 -> x0, waiting for transfers between devices: 71.4 us -> none  [body(): block = lax.all_gather(normed, 'section', axis=0, tiled=True)]
    all_gather x1 -> x0, blocking collectives: 43.1 us -> none  [body(): lax.all_gather(jnp.concatenate([norm_gain, router[None, :]], axis=0), 'ex...]
    dot_general x5 -> x1, matrix products: 40.7 us -> 6.63 us  [body(): lax.dot_general(place_own, back, (((0,), (0,)), ((), ())), preferred_elem...]
    unnamed x1 -> x0, blocking collectives: 27.4 us -> none
    all_to_all x2 -> x0, starting transfers between devices: 9.6 us -> none  [the longest x1 5 us: body(): lax.all_to_all(buffer, 'expert', split_axis=0, concat_axis=0, tiled=True)]
    all_to_all x2 -> x0, waiting for transfers between devices: 4.98 us -> none  [the longest x1 4.97 us: body(): lax.all_to_all(back, 'expert', split_axis=0, concat_axis=0, tiled=True)]
  transfers between devices with their start and end apart: 7 -> 2, of which waited for: 5 -> 0; matrix products, arithmetic and copies ran while one was open for 2% -> 5% of each run, Pallas kernels for 0% -> 90%
where the time goes in v2:
time: 194 us
  Pallas kernels  174 us (90%)
  matrix products  12.1 us (6%)
  other arithmetic  3.93 us (2%)
  starting transfers between devices  3.34 us (2%)
    pallas_call x1, Pallas kernels, exchanged(): pl.pallas_call(exchange_kernel, out_shape=jax.ShapeDtypeStruct(buffer.sha...  174 us
    dot_general x1, matrix products, body(): lax.dot_general(place_own, back, (((0,), (0,)), ((), ())), preferred_elem...  6.63 us
    dot_general x1, matrix products, body(): jnp.dot(place_ahead, activations, preferred_element_type=jnp.float32)  5.49 us
  transfers between devices with their start and end apart: 2, of which 0 were waited for; matrix products, arithmetic and copies ran while one was open for 5% of the time, Pallas kernels for 90%

profile of v2, /device:TPU:0, one launch (start us, length us, event | category | flops | bytes accessed | tf_op | source)
XLA Modules:
  0.0 193.8 jit_solution(8962825616212564546)
XLA Ops:
  0.0 0.5 collective-permute-start
  0.5 0.7 pad_add_fusion
  1.2 2.9 %collective-permute-start.1 = (s32[2,256]{1,0:T(2,128)S(1)}, s32[2,256]{1,0:T(2,128)S(1)}, u32[]{:S(2)}, u32[]{:S(2)}) collective-permute-start(s32[2,256]{1,0:T(2,128)S(1)} %pad_add_fusion), channel_id=1, source_target_pairs={{4,0},{8,4},{12,8},{16,12},{20,16},{24,20},{28,24},{0,28},{5,1},{9... | collective-permute-start | bytes 6152 | tf_op jit(solution)/shard_map/ppermute | solution.py:17
  4.0 0.1 pad.2.clone
  4.1 0.9 convert_reduce_fusion.1
  5.1 1.4 maximum_maximum_fusion.vectors
  6.5 0.7 multiply_add_fusion.1
  7.2 0.0 collective-permute-done.1
  7.2 0.2 convert_reduce_fusion
  7.4 5.5 %convolution_convert_fusion = bf16[384,2048]{1,0:T(8,128)(2,1)} fusion(bf16[1024,2048]{1,0:T(8,128)(2,1)} %param.9, s32[256]{0:T(256)S(1)} %bitcast.22, s32[256]{0:T(256)S(1)} %bitcast.21), kind=kOutput, calls=%fused_computation.1 | convolution fusion | flops 1813479424 | bytes 5769216 | tf_op jit(solution)/shard_map/dot_general | solution.py:360
  12.9 0.0 copy-start
  12.9 174.3 %shard_map.82 = bf16[4,96,2048]{2,1,0:T(8,128)(2,1)} custom-call(bf16[4,96,2048]{2,1,0:T(8,128)(2,1)} %bitcast.28, f32[8,2048]{1,0:T(8,128)} %maximum_maximum_fusion.vectors, bf16[384,8192]{1,0:T(8,128)(2,1)} %bitcast.24, bf16[384,8192]{1,0:T(8,128)(2,1)} %bitcast.25, bf16[384,8192]{1,0:T(8,128)(2,1)} %bitcast.26), custom_call_target="tpu_custom_call" | custom-call | flops 14495514624 | bytes 18874368 | tf_op jit(solution)/shard_map/pallas_call | solution.py:305
  187.2 0.0 collective-permute-done
  187.2 0.0 copy-done
  187.2 6.6 %add_convert_fusion = bf16[1024,2048]{1,0:T(8,128)(2,1)} fusion(bf16[1024,2048]{1,0:T(8,128)(2,1)} %collective-permute-done, bf16[384,2048]{1,0:T(8,128)(2,1)} %bitcast.27, s32[256]{0:T(256)S(1)} %bitcast.23, s32[256]{0:T(256)S(1)} %multiply_add_fusion.1), kind=kOutput, calls=%fused_computation | convolution fusion | flops 1818984448 | bytes 9963520 | tf_op jit(solution)/shard_map/dot_general | solution.py:367
  (3 shorter events, 0.0 us)
Async XLA Ops:
  0.0 187.2 %collective-permute-start = (bf16[1024,2048]{1,0:T(8,128)(2,1)}, bf16[1024,2048]{1,0:T(8,128)(2,1)}, u32[]{:S(2)}, u32[]{:S(2)}) collective-permute-start(bf16[1024,2048]{1,0:T(8,128)(2,1)} %param.9), channel_id=1, source_target_pairs={{28,0},{0,4},{4,8},{8,12},{12,16},{16,20},{20,24},{24,28},{29,1},{... | collective-permute-start | bytes 12582920 | tf_op jit(solution)/shard_map/ppermute | solution.py:17
  1.2 6.0 %collective-permute-start.1 = (s32[2,256]{1,0:T(2,128)S(1)}, s32[2,256]{1,0:T(2,128)S(1)}, u32[]{:S(2)}, u32[]{:S(2)}) collective-permute-start(s32[2,256]{1,0:T(2,128)S(1)} %pad_add_fusion), channel_id=1, source_target_pairs={{4,0},{8,4},{12,8},{16,12},{20,16},{24,20},{28,24},{0,28},{5,1},{9... | collective-permute-start | bytes 6152 | tf_op jit(solution)/shard_map/ppermute | solution.py:17
  12.9 174.3 %copy-start = (s32[1,256]{1,0:T(1,128)S(1)}, s32[1,256]{1,0:T(1,128)}, u32[]{:S(2)}) copy-start(s32[1,256]{1,0:T(1,128)} %param.10) | copy-start | bytes 3076

commit v3 on v2

--- a/solution.py
+++ b/solution.py
@@ -157,14 +157,14 @@
         def _(step):
             columns = pl.ds(pl.multiple_of(step * deep, deep), deep)
             block = gathered[pl.ds(first, 2 * cap), columns]
-            gate_sum[...] += feature_product(block, gate_v[:, columns])
-            up_sum[...] += feature_product(block, up_v[:, columns])
+            gate_sum[...] += feature_product(gate_v[:, columns], block)
+            up_sum[...] += feature_product(up_v[:, columns], block)
 
         marks = gathered[pl.ds(first, 2 * cap), full : full + LANES].astype(jnp.float32)
         score = jnp.sum(marks, axis=1, keepdims=True) * (2.0 / LANES)
         gate = gate_sum[...]
-        value = gate / (1.0 + jnp.exp(-gate)) * up_sum[...] * score
-        value = value.astype(jnp.bfloat16)
+        value = gate / (1.0 + jnp.exp(-gate)) * up_sum[...]
+        value = (value.T * score).astype(jnp.bfloat16)
         hidden[1, pl.ds(pl.multiple_of(owner_chip * cap, 16), cap), :] = value[:cap]
         after = lax.rem(owner_chip + 1, 4)
         hidden[0, pl.ds(pl.multiple_of(after * cap, 16), cap), :] = value[cap:]
@@ -314,8 +314,8 @@
             pltpu.VMEM((planes, cap, width), bf),
             pltpu.VMEM((planes,) + vectors.shape, jnp.float32),
             pltpu.VMEM((2 * chips * cap, full + LANES), bf),
-            pltpu.VMEM((2 * cap, hid), jnp.float32),
-            pltpu.VMEM((2 * cap, hid), jnp.float32),
+            pltpu.VMEM((hid, 2 * cap), jnp.float32),
+            pltpu.VMEM((hid, 2 * cap), jnp.float32),
             pltpu.VMEM((2, chips * cap, hid), bf),
             pltpu.VMEM((planes, chips * cap, width), bf),
             pltpu.VMEM((planes, chips * cap, width), bf),
@@ -355,8 +355,10 @@
     slots = expert_count * capacity
     ahead = passed_along(jnp.stack([picks, experts]), "section", -1)
     arrived = passed_along(activations, "section", 1)
-    place_ahead = slot_map(ahead[0], ahead[1], capacity, slots, tokens)
-    place_own = slot_map(picks, experts, capacity, slots, tokens)
+    place_own = lax.optimization_barrier(slot_map(picks, experts, capacity, slots, tokens))
+    place_ahead = lax.optimization_barrier(
+        slot_map(ahead[0], ahead[1], capacity, slots, tokens)
+    )
     buffer = jnp.dot(place_ahead, activations, preferred_element_type=jnp.float32)
     buffer = buffer.astype(jnp.bfloat16).reshape(planes, capacity, width)
     if (sections, planes) == (8, 4) and capacity % 32 == 0:

time: 194 us -> 194 us (level)
  Pallas kernels: 174 us -> 172 us
    pallas_call x1, Pallas kernels: 174 us -> 172 us  [exchanged(): pl.pallas_call(exchange_kernel, out_shape=jax.ShapeDtypeStruct(buffer.sha...]
  transfers between devices with their start and end apart: 2 -> 2, of which waited for: 0 -> 0; matrix products, arithmetic and copies ran while one was open for 5% -> 6% of each run, Pallas kernels for 90% -> 89%
where the time goes in v3:
time: 194 us; the launch traced here: 193 us
  Pallas kernels  172 us (89%)
  matrix products  13.9 us (7%)
  other arithmetic  3.93 us (2%)
  starting transfers between devices  3.34 us (2%)
    pallas_call x1, Pallas kernels, exchanged(): pl.pallas_call(exchange_kernel, out_shape=jax.ShapeDtypeStruct(buffer.sha...  172 us
    dot_general x1, matrix products, body(): lax.dot_general(place_own, back, (((0,), (0,)), ((), ())), preferred_elem...  7.07 us
    dot_general x1, matrix products, body(): jnp.dot(place_ahead, activations, preferred_element_type=jnp.float32)  5.13 us
  transfers between devices with their start and end apart: 2, of which 0 were waited for; matrix products, arithmetic and copies ran while one was open for 6% of the time, Pallas kernels for 89%

profile of v3, /device:TPU:0, one launch (start us, length us, event | category | flops | bytes accessed | tf_op | source)
XLA Modules:
  0.0 193.3 jit_solution(4865212026589051708)
XLA Ops:
  0.0 0.5 collective-permute-start
  0.5 0.7 pad_add_fusion
  1.2 2.9 %collective-permute-start.1 = (s32[2,256]{1,0:T(2,128)S(1)}, s32[2,256]{1,0:T(2,128)S(1)}, u32[]{:S(2)}, u32[]{:S(2)}) collective-permute-start(s32[2,256]{1,0:T(2,128)S(1)} %pad_add_fusion), channel_id=1, source_target_pairs={{4,0},{8,4},{12,8},{16,12},{20,16},{24,20},{28,24},{0,28},{5,1},{9... | collective-permute-start | bytes 6152 | tf_op jit(solution)/shard_map/ppermute | solution.py:17
  4.0 0.1 pad.2.clone
  4.1 0.9 convert_reduce_fusion.1
  5.1 0.7 multiply_add_fusion.1
  5.7 1.4 maximum_maximum_fusion.vectors
  7.2 1.2 convolution_convert_fusion.2
  8.4 0.0 collective-permute-done.1
  8.4 0.2 convert_reduce_fusion
  8.6 0.5 convolution_convert_fusion.1
  9.1 5.1 %convolution_convert_fusion = bf16[384,2048]{1,0:T(8,128)(2,1)} fusion(bf16[384,1024]{1,0:T(8,128)(2,1)S(1)} %convolution_convert_fusion.1, bf16[1024,2048]{1,0:T(8,128)(2,1)} %param.9), kind=kOutput, calls=%fused_computation.1 | convolution fusion | flops 1611399168 | bytes 6553600 | tf_op jit(solution)/shard_map/dot_general | solution.py:362
  14.3 172.0 %shard_map.82 = bf16[4,96,2048]{2,1,0:T(8,128)(2,1)} custom-call(bf16[4,96,2048]{2,1,0:T(8,128)(2,1)} %bitcast.30, f32[8,2048]{1,0:T(8,128)} %maximum_maximum_fusion.vectors, bf16[384,8192]{1,0:T(8,128)(2,1)} %bitcast.26, bf16[384,8192]{1,0:T(8,128)(2,1)} %bitcast.27, bf16[384,8192]{1,0:T(8,128)(2,1)} %bitcast.28), custom_call_target="tpu_custom_call" | custom-call | flops 14495514624 | bytes 18874368 | tf_op jit(solution)/shard_map/pallas_call | solution.py:305
  186.2 0.0 collective-permute-done
  186.2 7.1 %add_convert_fusion = bf16[1024,2048]{1,0:T(8,128)(2,1)} fusion(bf16[1024,2048]{1,0:T(8,128)(2,1)} %collective-permute-done, bf16[384,1024]{1,0:T(8,128)(2,1)S(1)} %convolution_convert_fusion.2, bf16[384,2048]{1,0:T(8,128)(2,1)} %bitcast.29), kind=kOutput, calls=%fused_computation | convolution fusion | flops 1616904192 | bytes 10747904 | tf_op jit(solution)/shard_map/dot_general | solution.py:369
  (3 shorter events, 0.0 us)
Async XLA Ops:
  0.0 186.2 %collective-permute-start = (bf16[1024,2048]{1,0:T(8,128)(2,1)}, bf16[1024,2048]{1,0:T(8,128)(2,1)}, u32[]{:S(2)}, u32[]{:S(2)}) collective-permute-start(bf16[1024,2048]{1,0:T(8,128)(2,1)} %param.9), channel_id=1, source_target_pairs={{28,0},{0,4},{4,8},{8,12},{12,16},{16,20},{20,24},{24,28},{29,1},{... | collective-permute-start | bytes 12582920 | tf_op jit(solution)/shard_map/ppermute | solution.py:17
  1.2 7.2 %collective-permute-start.1 = (s32[2,256]{1,0:T(2,128)S(1)}, s32[2,256]{1,0:T(2,128)S(1)}, u32[]{:S(2)}, u32[]{:S(2)}) collective-permute-start(s32[2,256]{1,0:T(2,128)S(1)} %pad_add_fusion), channel_id=1, source_target_pairs={{4,0},{8,4},{12,8},{16,12},{20,16},{24,20},{28,24},{0,28},{5,1},{9... | collective-permute-start | bytes 6152 | tf_op jit(solution)/shard_map/ppermute | solution.py:17

commit v4 on v3

--- a/solution.py
+++ b/solution.py
@@ -39,10 +39,11 @@
 
 
 def exchange_kernel(
-    rows_in, vectors, gate_hbm, up_hbm, down_hbm, out,
+    rows_in, vectors, gate_hbm, up_hbm, down_hbm, leaving, out, arrived,
     gate_v, up_v, down_v, came, vec, gathered, gate_sum, up_sum, hidden,
     for_sib, mine, from_sib, relay_x, relay_y, final_x, final_y, done,
     load_sem, z_send, z_recv, vec_send, vec_recv, ag_send, ag_recv, rs_send, rs_recv, back_send, back_recv,
+    shift_send, shift_recv,
 ):
     planes, cap, width = rows_in.shape
     full = planes * width
@@ -57,8 +58,12 @@
     dests = {"x": (xn, plane), "y": (yn, plane), "s": (sib, plane)}
     uppers = [lax.rem(plane + j, planes) for j in range(1, planes)]
 
+    sections = lax.axis_size("section")
+    following, previous = lax.rem(me + 1, sections), lax.rem(me + sections - 1, sections)
+
     barrier = pltpu.get_barrier_semaphore()
     greeted = list(dests.values()) + [(me, p) for p in uppers]
+    greeted += [(following, plane), (previous, plane)]
     for device in greeted:
         pl.semaphore_signal(barrier, inc=1, device_id=device, device_id_type=MESH)
     pl.semaphore_wait(barrier, len(greeted))
@@ -73,19 +78,32 @@
         copy.start()
         sent.append(copy)
         return copy
+
+    early = leaving.shape[0] * 5 // 8
+    parts = [pl.ds(0, early), pl.ds(early, leaving.shape[0] - early)]
+
+    def shift(n):
+        return send(
+            leaving.at[parts[n]], arrived.at[parts[n]],
+            shift_send.at[n], shift_recv.at[n], (following, plane),
+        )
 
     z_copies = {}
     vec_copies = [
         send(vectors, vec.at[plane], vec_send.at[j], vec_recv.at[j], (me, p))
         for j, p in enumerate(uppers)
     ]
-    for part in range(2):
+
+    def to_planes(part):
         piece = pl.ds(part * half, half)
         for j, p in enumerate(uppers):
             n = part * (planes - 1) + j
             z_copies[part, j] = send(
                 rows_in.at[p, piece], came.at[plane, piece], z_send.at[n], z_recv.at[n], (me, p)
             )
+
+    to_planes(0)
+    shifts = [shift(0)]
     local = [
         pltpu.make_async_copy(rows_in.at[plane], came.at[plane], load_sem.at[0]),
         pltpu.make_async_copy(vectors, vec.at[plane], load_sem.at[1]),
@@ -95,6 +113,10 @@
     ]
     for copy in local:
         copy.start()
+    for j in range(planes - 1):
+        z_copies[0, j].wait_send()
+    sent[:] = [copy for copy in sent if all(copy is not z_copies[0, j] for j in range(planes - 1))]
+    to_planes(1)
 
     def place(owner_chip, owner_core, part):
         return pl.ds(
@@ -194,6 +216,7 @@
     products(chip_y)
     ag["fx"].wait_recv()
     pass_block("sd1", chip_d, 1, "s")
+    shifts.append(shift(1))
     ag["sd0"].wait_recv()
     ag["sd1"].wait_recv()
     products(chip_d)
@@ -292,11 +315,13 @@
     for copy in back:
         copy.wait_recv()
     own.wait()
+    for copy in shifts:
+        copy.wait_recv()
     for copy in sent:
         copy.wait_send()
 
 
-def exchanged(buffer, vectors, gate, up, down):
+def exchanged(buffer, vectors, gate, up, down, leaving):
     planes, cap, width = buffer.shape
     hid, full = gate.shape
     half, chips = cap // 2, 4
@@ -304,9 +329,12 @@
     anywhere = pl.BlockSpec(memory_space=pl.ANY)
     return pl.pallas_call(
         exchange_kernel,
-        out_shape=jax.ShapeDtypeStruct(buffer.shape, bf),
-        in_specs=[anywhere] * 5,
-        out_specs=anywhere,
+        out_shape=[
+            jax.ShapeDtypeStruct(buffer.shape, bf),
+            jax.ShapeDtypeStruct(leaving.shape, bf),
+        ],
+        in_specs=[anywhere] * 6,
+        out_specs=[anywhere] * 2,
         scratch_shapes=[
             pltpu.VMEM((hid, full), bf),
             pltpu.VMEM((hid, full), bf),
@@ -336,6 +364,8 @@
             dma((7 * planes,)),
             dma((planes - 1,)),
             dma((planes - 1,)),
+            dma((2,)),
+            dma((2,)),
         ],
         compiler_params=pltpu.CompilerParams(
             collective_id=0, has_side_effects=True, vmem_limit_bytes=63 * 1024 * 1024
@@ -343,7 +373,7 @@
         cost_estimate=pl.CostEstimate(
             flops=6 * 2 * chips * cap * hid * full, bytes_accessed=6 * hid * full, transcendentals=0
         ),
-    )(buffer, vectors, gate, up, down)
+    )(buffer, vectors, gate, up, down, leaving)
 
 
 def body(activations, modality, selected, routes, norm_gain, router, gate_w, up_w, down_w):
@@ -354,7 +384,6 @@
     capacity = max(2, 3 * picks.shape[0] // (2 * expert_count))
     slots = expert_count * capacity
     ahead = passed_along(jnp.stack([picks, experts]), "section", -1)
-    arrived = passed_along(activations, "section", 1)
     place_own = lax.optimization_barrier(slot_map(picks, experts, capacity, slots, tokens))
     place_ahead = lax.optimization_barrier(
         slot_map(ahead[0], ahead[1], capacity, slots, tokens)
@@ -365,11 +394,14 @@
         vectors = jnp.concatenate(
             [norm_gain, router[None, :], jnp.zeros((5, width), jnp.float32)], axis=0
         )
-        back = exchanged(buffer, vectors, gate_w[0], up_w[0], down_w[0]).reshape(slots, width)
+        back, arrived = exchanged(
+            buffer, vectors, gate_w[0], up_w[0], down_w[0], activations
+        )
         added = lax.dot_general(
-            place_own, back, (((0,), (0,)), ((), ())), preferred_element_type=jnp.float32
+            place_own, back.reshape(slots, width), (((0,), (0,)), ((), ())), preferred_element_type=jnp.float32
         )
         return (arrived.astype(jnp.float32) + added).astype(jnp.bfloat16)
+    arrived = passed_along(activations, "section", 1)
     whole = lax.all_gather(
         jnp.concatenate([norm_gain, router[None, :]], axis=0), "expert", axis=1, tiled=True
     )

time: 194 us -> 192 us (0.990); the launches traced: 193 us -> 189 us
  Pallas kernels: 172 us -> 168 us
    pallas_call x1, Pallas kernels: 172 us -> 168 us  [exchanged(): pl.pallas_call(exchange_kernel, out_shape=[jax.ShapeDtypeStruct(buffer.sh...]
  transfers between devices with their start and end apart: 2 -> 1, of which waited for: 0 -> 0; matrix products, arithmetic and copies ran while one was open for 6% -> 2% of each run, Pallas kernels for 89% -> 0%
where the time goes in v4:
time: 192 us; the launch traced here: 189 us
  Pallas kernels  168 us (88%)
  matrix products  13.9 us (7%)
  other arithmetic  3.93 us (2%)
  starting transfers between devices  3.33 us (2%)
    pallas_call x1, Pallas kernels, exchanged(): pl.pallas_call(exchange_kernel, out_shape=[jax.ShapeDtypeStruct(buffer.sh...  168 us
    dot_general x1, matrix products, body(): lax.dot_general(place_own, back.reshape(slots, width), (((0,), (0,)), (()...  7.07 us
    dot_general x1, matrix products, body(): jnp.dot(place_ahead, activations, preferred_element_type=jnp.float32)  5.13 us
  transfers between devices with their start and end apart: 1, of which 0 were waited for; matrix products, arithmetic and copies ran while one was open for 2% of the time, Pallas kernels for 0%

profile of v4, /device:TPU:0, one launch (start us, length us, event | category | flops | bytes accessed | tf_op | source)
XLA Modules:
  0.0 189.3 jit_solution(5383393676716362669)
XLA Ops:
  0.0 0.7 pad_add_fusion
  0.7 3.3 %collective-permute-start = (s32[2,256]{1,0:T(2,128)S(1)}, s32[2,256]{1,0:T(2,128)S(1)}, u32[]{:S(2)}, u32[]{:S(2)}) collective-permute-start(s32[2,256]{1,0:T(2,128)S(1)} %pad_add_fusion), channel_id=1, source_target_pairs={{4,0},{8,4},{12,8},{16,12},{20,16},{24,20},{28,24},{0,28},{5,1},{9... | collective-permute-start | bytes 6152 | tf_op jit(solution)/shard_map/ppermute | solution.py:17
  4.0 0.9 convert_reduce_fusion
  5.0 0.7 multiply_add_fusion
  5.7 0.1 pad.2.clone
  5.7 1.4 maximum_maximum_fusion.vectors
  7.2 1.2 convolution_convert_fusion.1
  8.4 0.0 collective-permute-done
  8.4 0.2 convert_reduce_fusion.1
  8.6 0.5 convolution_convert_fusion.2
  9.1 5.1 %convolution_convert_fusion = bf16[384,2048]{1,0:T(8,128)(2,1)} fusion(bf16[384,1024]{1,0:T(8,128)(2,1)S(1)} %convolution_convert_fusion.2, bf16[1024,2048]{1,0:T(8,128)(2,1)} %leaving.1), kind=kOutput, calls=%fused_computation.1 | convolution fusion | flops 1611399168 | bytes 6553600 | tf_op jit(solution)/shard_map/dot_general | solution.py:391
  14.3 167.9 %shard_map.82 = (bf16[4,96,2048]{2,1,0:T(8,128)(2,1)}, bf16[1024,2048]{1,0:T(8,128)(2,1)}) custom-call(bf16[4,96,2048]{2,1,0:T(8,128)(2,1)} %bitcast.30, f32[8,2048]{1,0:T(8,128)} %maximum_maximum_fusion.vectors, bf16[384,8192]{1,0:T(8,128)(2,1)} %bitcast.26, bf16[384,8192]{1,0:T(8,128)(2,1)} %bitcast.27, bf16[384,8192]{1,0:T(8,128)(2,1)} %bitcast.28, ...), custom_call_target="tpu_custom_call" | custom-call | flops 14495514624 | bytes 18874368 | tf_op jit(solution)/shard_map/pallas_call | solution.py:330
  182.2 7.1 %add_convert_fusion = bf16[1024,2048]{1,0:T(8,128)(2,1)} fusion(bf16[1024,2048]{1,0:T(8,128)(2,1)} %get-tuple-element.7, bf16[384,1024]{1,0:T(8,128)(2,1)S(1)} %convolution_convert_fusion.1, bf16[384,2048]{1,0:T(8,128)(2,1)} %bitcast.29), kind=kOutput, calls=%fused_computation | convolution fusion | flops 1616904192 | bytes 10747904 | tf_op jit(solution)/shard_map/dot_general | solution.py:400
  (3 shorter events, 0.0 us)
Async XLA Ops:
  0.7 7.7 %collective-permute-start = (s32[2,256]{1,0:T(2,128)S(1)}, s32[2,256]{1,0:T(2,128)S(1)}, u32[]{:S(2)}, u32[]{:S(2)}) collective-permute-start(s32[2,256]{1,0:T(2,128)S(1)} %pad_add_fusion), channel_id=1, source_target_pairs={{4,0},{8,4},{12,8},{16,12},{20,16},{24,20},{28,24},{0,28},{5,1},{9... | collective-permute-start | bytes 6152 | tf_op jit(solution)/shard_map/ppermute | solution.py:17

commit v5 on v4

--- a/solution.py
+++ b/solution.py
@@ -223,18 +223,21 @@
     local[4].wait()
 
     rs = {}
-    targets = [lax.rem(plane + 1 + i, planes) for i in range(planes)]
+    steps, span = mine.shape[0], mine.shape[2]
+    halves = steps // planes
+    targets = [lax.rem(plane + 1 + i // halves, planes) for i in range(steps)]
 
     def give(kind, n, i, src, dst, to):
-        at = n * planes + i
+        at = n * steps + i
         rs[kind, i] = send(src, dst, rs_send.at[at], rs_recv.at[at], dests[to])
 
     def down(i, which, into):
         wide = 512
 
-        @pl.loop(0, width // wide)
+        @pl.loop(0, span // wide)
         def _(step):
-            columns = pl.ds(pl.multiple_of(targets[i] * width + step * wide, wide), wide)
+            start = targets[i] * width + i % halves * span + step * wide
+            columns = pl.ds(pl.multiple_of(start, wide), wide)
             to = pl.ds(pl.multiple_of(step * wide, wide), wide)
             into[i, :, to] = jnp.dot(
                 hidden[which], down_v[:, columns], preferred_element_type=jnp.float32
@@ -243,6 +246,8 @@
     def start_sums(i):
         down(i, 1 - core, for_sib)
         give("s", 0, i, for_sib.at[i], from_sib.at[i], "s")
+
+    def own_sums(i):
         down(i, core, mine)
 
     def add_into(ref, i, first, count, others):
@@ -282,39 +287,38 @@
         add_into(None, i, first, half, [(relay_y, 0)])
         give("x1", 6, i, mine.at[i, pl.ds(first, half)], final_x.at[i, pl.ds(half, half)], "x")
 
-    back = []
+    back, own = [], []
 
     def final_sums(i):
         for kind in ("x0", "y1", "y0", "x1"):
             rs[kind, i].wait_recv()
         base = pl.multiple_of(chip * cap, 16)
         add_into(done, i, base, cap, [(from_sib, base), (final_x, 0), (final_y, 0)])
-        if i < planes - 1:
-            back.append(
-                send(done.at[i], out.at[plane], back_send.at[i], back_recv.at[i], (me, targets[i]))
-            )
+        to = out.at[plane, :, pl.ds(i % halves * span, span)]
+        if i < steps - halves:
+            back.append(send(done.at[i], to, back_send.at[i], back_recv.at[i], (me, targets[i])))
+        else:
+            copy = pltpu.make_async_copy(done.at[i], to, load_sem.at[5 + i - (steps - halves)])
+            copy.start()
+            own.append(copy)
 
     start_sums(0)
-    start_sums(1)
-    chip_sums(0)
-    start_sums(2)
-    start_sums(3)
-    chip_sums(1)
-    relay_sums(0)
-    chip_sums(2)
-    relay_sums(1)
-    final_sums(0)
-    chip_sums(3)
-    relay_sums(2)
-    final_sums(1)
-    relay_sums(3)
-    final_sums(2)
-    final_sums(3)
-    own = pltpu.make_async_copy(done.at[planes - 1], out.at[plane], load_sem.at[5])
-    own.start()
+    own_sums(0)
+    for i in range(steps + 3):
+        if i + 1 < steps:
+            start_sums(i + 1)
+        if i < steps:
+            chip_sums(i)
+        if i + 1 < steps:
+            own_sums(i + 1)
+        if 0 <= i - 2 < steps:
+            relay_sums(i - 2)
+        if 0 <= i - 3 < steps:
+            final_sums(i - 3)
     for copy in back:
         copy.wait_recv()
-    own.wait()
+    for copy in own:
+        copy.wait()
     for copy in shifts:
         copy.wait_recv()
     for copy in sent:
@@ -324,7 +328,8 @@
 def exchanged(buffer, vectors, gate, up, down, leaving):
     planes, cap, width = buffer.shape
     hid, full = gate.shape
-    half, chips = cap // 2, 4
+    half, chips, halves = cap // 2, 4, 2
+    steps, span = planes * halves, width // halves
     bf, dma = jnp.bfloat16, pltpu.SemaphoreType.DMA
     anywhere = pl.BlockSpec(memory_space=pl.ANY)
     return pl.pallas_call(
@@ -345,25 +350,25 @@
             pltpu.VMEM((hid, 2 * cap), jnp.float32),
             pltpu.VMEM((hid, 2 * cap), jnp.float32),
             pltpu.VMEM((2, chips * cap, hid), bf),
-            pltpu.VMEM((planes, chips * cap, width), bf),
-            pltpu.VMEM((planes, chips * cap, width), bf),
-            pltpu.VMEM((planes, chips * cap, width), bf),
-            pltpu.VMEM((planes, half, width), bf),
-            pltpu.VMEM((planes, half, width), bf),
-            pltpu.VMEM((planes, cap, width), bf),
-            pltpu.VMEM((planes, cap, width), bf),
-            pltpu.VMEM((planes, cap, width), bf),
-            dma((6,)),
+            pltpu.VMEM((steps, chips * cap, span), bf),
+            pltpu.VMEM((steps, chips * cap, span), bf),
+            pltpu.VMEM((steps, chips * cap, span), bf),
+            pltpu.VMEM((steps, half, span), bf),
+            pltpu.VMEM((steps, half, span), bf),
+            pltpu.VMEM((steps, cap, span), bf),
+            pltpu.VMEM((steps, cap, span), bf),
+            pltpu.VMEM((steps, cap, span), bf),
+            dma((5 + halves,)),
             dma((2 * (planes - 1),)),
             dma((2 * (planes - 1),)),
             dma((planes - 1,)),
             dma((planes - 1,)),
             dma((14,)),
             dma((14,)),
-            dma((7 * planes,)),
-            dma((7 * planes,)),
-            dma((planes - 1,)),
-            dma((planes - 1,)),
+            dma((7 * steps,)),
+            dma((7 * steps,)),
+            dma((steps - halves,)),
+            dma((steps - halves,)),
             dma((2,)),
             dma((2,)),
         ],

time: 192 us -> 189 us (0.984)
  Pallas kernels: 168 us -> 165 us
    pallas_call x1, Pallas kernels: 168 us -> 165 us  [exchanged(): pl.pallas_call(exchange_kernel, out_shape=[jax.ShapeDtypeStruct(buffer.sh...]
where the time goes in v5:
time: 189 us; the launch traced here: 187 us
  Pallas kernels  165 us (87%)
  matrix products  13.9 us (7%)
  other arithmetic  3.93 us (2%)
  starting transfers between devices  3.33 us (2%)
    pallas_call x1, Pallas kernels, exchanged(): pl.pallas_call(exchange_kernel, out_shape=[jax.ShapeDtypeStruct(buffer.sh...  165 us
    dot_general x1, matrix products, body(): lax.dot_general(place_own, back.reshape(slots, width), (((0,), (0,)), (()...  7.07 us
    dot_general x1, matrix products, body(): jnp.dot(place_ahead, activations, preferred_element_type=jnp.float32)  5.13 us
  transfers between devices with their start and end apart: 1, of which 0 were waited for; matrix products, arithmetic and copies ran while one was open for 2% of the time, Pallas kernels for 0%

profile of v5, /device:TPU:0, one launch (start us, length us, event | category | flops | bytes accessed | tf_op | source)
XLA Modules:
  0.0 186.7 jit_solution(16978196210503696902)
XLA Ops:
  0.0 0.7 pad_add_fusion
  0.7 3.3 %collective-permute-start = (s32[2,256]{1,0:T(2,128)S(1)}, s32[2,256]{1,0:T(2,128)S(1)}, u32[]{:S(2)}, u32[]{:S(2)}) collective-permute-start(s32[2,256]{1,0:T(2,128)S(1)} %pad_add_fusion), channel_id=1, source_target_pairs={{4,0},{8,4},{12,8},{16,12},{20,16},{24,20},{28,24},{0,28},{5,1},{9... | collective-permute-start | bytes 6152 | tf_op jit(solution)/shard_map/ppermute | solution.py:17
  4.0 0.9 convert_reduce_fusion
  5.0 0.7 multiply_add_fusion
  5.7 0.1 pad.2.clone
  5.7 1.4 maximum_maximum_fusion.vectors
  7.2 1.2 convolution_convert_fusion.1
  8.4 0.0 collective-permute-done
  8.4 0.2 convert_reduce_fusion.1
  8.6 0.5 convolution_convert_fusion.2
  9.1 5.1 %convolution_convert_fusion = bf16[384,2048]{1,0:T(8,128)(2,1)} fusion(bf16[384,1024]{1,0:T(8,128)(2,1)S(1)} %convolution_convert_fusion.2, bf16[1024,2048]{1,0:T(8,128)(2,1)} %leaving.1), kind=kOutput, calls=%fused_computation.1 | convolution fusion | flops 1611399168 | bytes 6553600 | tf_op jit(solution)/shard_map/dot_general | solution.py:396
  14.3 165.3 %shard_map.82 = (bf16[4,96,2048]{2,1,0:T(8,128)(2,1)}, bf16[1024,2048]{1,0:T(8,128)(2,1)}) custom-call(bf16[4,96,2048]{2,1,0:T(8,128)(2,1)} %bitcast.30, f32[8,2048]{1,0:T(8,128)} %maximum_maximum_fusion.vectors, bf16[384,8192]{1,0:T(8,128)(2,1)} %bitcast.26, bf16[384,8192]{1,0:T(8,128)(2,1)} %bitcast.27, bf16[384,8192]{1,0:T(8,128)(2,1)} %bitcast.28, ...), custom_call_target="tpu_custom_call" | custom-call | flops 14495514624 | bytes 18874368 | tf_op jit(solution)/shard_map/pallas_call | solution.py:335
  179.6 7.1 %add_convert_fusion = bf16[1024,2048]{1,0:T(8,128)(2,1)} fusion(bf16[1024,2048]{1,0:T(8,128)(2,1)} %get-tuple-element.7, bf16[384,1024]{1,0:T(8,128)(2,1)S(1)} %convolution_convert_fusion.1, bf16[384,2048]{1,0:T(8,128)(2,1)} %bitcast.29), kind=kOutput, calls=%fused_computation | convolution fusion | flops 1616904192 | bytes 10747904 | tf_op jit(solution)/shard_map/dot_general | solution.py:405
  (3 shorter events, 0.0 us)
Async XLA Ops:
  0.7 7.7 %collective-permute-start = (s32[2,256]{1,0:T(2,128)S(1)}, s32[2,256]{1,0:T(2,128)S(1)}, u32[]{:S(2)}, u32[]{:S(2)}) collective-permute-start(s32[2,256]{1,0:T(2,128)S(1)} %pad_add_fusion), channel_id=1, source_target_pairs={{4,0},{8,4},{12,8},{16,12},{20,16},{24,20},{28,24},{0,28},{5,1},{9... | collective-permute-start | bytes 6152 | tf_op jit(solution)/shard_map/ppermute | solution.py:17

commit v6 on v5

--- a/solution.py
+++ b/solution.py
@@ -48,6 +48,8 @@
     planes, cap, width = rows_in.shape
     full = planes * width
     half = cap // 2
+    thin = 16
+    pieces = cap // thin
     hid = gate_hbm.shape[0]
     me, plane = lax.axis_index("section"), lax.axis_index("expert")
     core, chip = lax.rem(me, 2), lax.div(me, 2)
@@ -95,7 +97,7 @@
     ]
 
     def to_planes(part):
-        piece = pl.ds(part * half, half)
+        piece = pl.ds(part * thin, thin)
         for j, p in enumerate(uppers):
             n = part * (planes - 1) + j
             z_copies[part, j] = send(
@@ -113,23 +115,19 @@
     ]
     for copy in local:
         copy.start()
-    for j in range(planes - 1):
-        z_copies[0, j].wait_send()
-    sent[:] = [copy for copy in sent if all(copy is not z_copies[0, j] for j in range(planes - 1))]
-    to_planes(1)
 
     def place(owner_chip, owner_core, part):
         return pl.ds(
-            pl.multiple_of((owner_chip * 2 + owner_core) * cap + part * half, 16), half
+            pl.multiple_of((owner_chip * 2 + owner_core) * cap + part * thin, 16), thin
         )
 
     image = (plane >= planes // 2).astype(jnp.float32)
 
     def norm(part):
-        @pl.loop(0, half // 16)
+        @pl.loop(0, thin // 16)
         def _(step):
-            at = pl.ds(pl.multiple_of(part * half + step * 16, 16), 16)
-            to = pl.ds(pl.multiple_of(me * cap + part * half + step * 16, 16), 16)
+            at = pl.ds(pl.multiple_of(part * thin + step * 16, 16), 16)
+            to = pl.ds(pl.multiple_of(me * cap + part * thin + step * 16, 16), 16)
             squares = jnp.zeros((16, 1), jnp.float32)
             terms = jnp.zeros((16, 1), jnp.float32)
             for q in range(planes):
@@ -150,24 +148,52 @@
             ).astype(jnp.bfloat16)
 
     ag = {}
-    names = ["x0", "x1", "y0", "y1", "fx", "fy", "s0", "s1", "sx0", "sx1", "sy0", "sy1", "sd0", "sd1"]
-
-    def pass_block(name, owner_chip, part, to):
+    kinds = ["x", "y", "f", "s", "sx", "sy", "sd"]
+
+    def pass_block(kind, owner_chip, part, to):
         ref = gathered.at[place(owner_chip, core, part)]
-        n = names.index(name)
-        ag[name] = send(ref, ref, ag_send.at[n], ag_recv.at[n], dests[to])
+        n = kinds.index(kind) * pieces + part
+        ag[kind, part] = send(ref, ref, ag_send.at[n], ag_recv.at[n], dests[to])
 
     local[0].wait()
     local[1].wait()
     for copy in vec_copies:
         copy.wait_recv()
-    for part in range(2):
+
+    def forward(part):
+        ag["x", part].wait_recv()
+        if part % 2 == 0:
+            pass_block("f", chip_x, part, "y")
+        pass_block("sx", chip_x, part, "s")
+        ag["y", part].wait_recv()
+        if part % 2 == 1:
+            pass_block("f", chip_y, part, "x")
+        pass_block("sy", chip_y, part, "s")
+
+    def forward_last(part):
+        ag["f", part].wait_recv()
+        pass_block("sd", chip_d, part, "s")
+
+    def wait_all(kind):
+        for part in range(pieces):
+            ag[kind, part].wait_recv()
+
+    for part in range(pieces):
+        for j in range(planes - 1):
+            z_copies[part, j].wait_send()
+        if part + 1 < pieces:
+            to_planes(part + 1)
         for j in range(planes - 1):
             z_copies[part, j].wait_recv()
         norm(part)
-        pass_block(f"x{part}", chip, part, "x")
-        pass_block(f"y{part}", chip, part, "y")
-        pass_block(f"s{part}", chip, part, "s")
+        pass_block("x", chip, part, "x")
+        pass_block("y", chip, part, "y")
+        pass_block("s", chip, part, "s")
+        if part >= 1:
+            forward(part - 1)
+    forward(pieces - 1)
+    gone = [id(copy) for copy in z_copies.values()]
+    sent[:] = [copy for copy in sent if id(copy) not in gone]
 
     def products(owner_chip):
         first = pl.multiple_of(owner_chip * 2 * cap, 16)
@@ -191,34 +217,20 @@
         after = lax.rem(owner_chip + 1, 4)
         hidden[0, pl.ds(pl.multiple_of(after * cap, 16), cap), :] = value[cap:]
 
-    ag["x0"].wait_recv()
-    pass_block("fy", chip_x, 0, "y")
-    pass_block("sx0", chip_x, 0, "s")
-    ag["y0"].wait_recv()
-    pass_block("sy0", chip_y, 0, "s")
-    ag["s0"].wait_recv()
-    ag["s1"].wait_recv()
+    wait_all("s")
     local[2].wait()
     local[3].wait()
     products(chip)
-    ag["y1"].wait_recv()
-    pass_block("fx", chip_y, 1, "x")
-    pass_block("sy1", chip_y, 1, "s")
-    ag["x1"].wait_recv()
-    pass_block("sx1", chip_x, 1, "s")
-    ag["sx0"].wait_recv()
-    ag["sx1"].wait_recv()
+    for part in range(pieces - 2):
+        forward_last(part)
+    wait_all("sx")
     products(chip_x)
-    ag["fy"].wait_recv()
-    pass_block("sd0", chip_d, 0, "s")
-    ag["sy0"].wait_recv()
-    ag["sy1"].wait_recv()
+    forward_last(pieces - 2)
+    wait_all("sy")
     products(chip_y)
-    ag["fx"].wait_recv()
-    pass_block("sd1", chip_d, 1, "s")
+    forward_last(pieces - 1)
     shifts.append(shift(1))
-    ag["sd0"].wait_recv()
-    ag["sd1"].wait_recv()
+    wait_all("sd")
     products(chip_d)
     local[4].wait()
 
@@ -359,12 +371,12 @@
             pltpu.VMEM((steps, cap, span), bf),
             pltpu.VMEM((steps, cap, span), bf),
             dma((5 + halves,)),
-            dma((2 * (planes - 1),)),
-            dma((2 * (planes - 1),)),
+            dma((cap // 16 * (planes - 1),)),
+            dma((cap // 16 * (planes - 1),)),
             dma((planes - 1,)),
             dma((planes - 1,)),
-            dma((14,)),
-            dma((14,)),
+            dma((7 * cap // 16,)),
+            dma((7 * cap // 16,)),
             dma((7 * steps,)),
             dma((7 * steps,)),
             dma((steps - halves,)),

time: 189 us -> 193 us (1.021)
  Pallas kernels: 165 us -> 170 us
    pallas_call x1, Pallas kernels: 165 us -> 170 us  [exchanged(): pl.pallas_call(exchange_kernel, out_shape=[jax.ShapeDtypeStruct(buffer.sh...]
where the time goes in v6:
time: 193 us; the launch traced here: 191 us
  Pallas kernels  170 us (88%)
  matrix products  13.9 us (7%)
  other arithmetic  3.93 us (2%)
  starting transfers between devices  3.33 us (2%)
    pallas_call x1, Pallas kernels, exchanged(): pl.pallas_call(exchange_kernel, out_shape=[jax.ShapeDtypeStruct(buffer.sh...  170 us
    dot_general x1, matrix products, body(): lax.dot_general(place_own, back.reshape(slots, width), (((0,), (0,)), (()...  7.07 us
    dot_general x1, matrix products, body(): jnp.dot(place_ahead, activations, preferred_element_type=jnp.float32)  5.13 us
  transfers between devices with their start and end apart: 1, of which 0 were waited for; matrix products, arithmetic and copies ran while one was open for 2% of the time, Pallas kernels for 0%

profile of v6, /device:TPU:0, one launch (start us, length us, event | category | flops | bytes accessed | tf_op | source)
XLA Modules:
  0.0 191.0 jit_solution(6440843759776964505)
XLA Ops:
  0.0 0.7 pad_add_fusion
  0.7 3.3 %collective-permute-start = (s32[2,256]{1,0:T(2,128)S(1)}, s32[2,256]{1,0:T(2,128)S(1)}, u32[]{:S(2)}, u32[]{:S(2)}) collective-permute-start(s32[2,256]{1,0:T(2,128)S(1)} %pad_add_fusion), channel_id=1, source_target_pairs={{4,0},{8,4},{12,8},{16,12},{20,16},{24,20},{28,24},{0,28},{5,1},{9... | collective-permute-start | bytes 6152 | tf_op jit(solution)/shard_map/ppermute | solution.py:17
  4.0 0.9 convert_reduce_fusion
  5.0 0.7 multiply_add_fusion
  5.7 0.1 pad.2.clone
  5.7 1.4 maximum_maximum_fusion.vectors
  7.2 1.2 convolution_convert_fusion.1
  8.4 0.0 collective-permute-done
  8.4 0.2 convert_reduce_fusion.1
  8.6 0.5 convolution_convert_fusion.2
  9.1 5.1 %convolution_convert_fusion = bf16[384,2048]{1,0:T(8,128)(2,1)} fusion(bf16[384,1024]{1,0:T(8,128)(2,1)S(1)} %convolution_convert_fusion.2, bf16[1024,2048]{1,0:T(8,128)(2,1)} %leaving.1), kind=kOutput, calls=%fused_computation.1 | convolution fusion | flops 1611399168 | bytes 6553600 | tf_op jit(solution)/shard_map/dot_general | solution.py:408
  14.3 169.7 %shard_map.82 = (bf16[4,96,2048]{2,1,0:T(8,128)(2,1)}, bf16[1024,2048]{1,0:T(8,128)(2,1)}) custom-call(bf16[4,96,2048]{2,1,0:T(8,128)(2,1)} %bitcast.30, f32[8,2048]{1,0:T(8,128)} %maximum_maximum_fusion.vectors, bf16[384,8192]{1,0:T(8,128)(2,1)} %bitcast.26, bf16[384,8192]{1,0:T(8,128)(2,1)} %bitcast.27, bf16[384,8192]{1,0:T(8,128)(2,1)} %bitcast.28, ...), custom_call_target="tpu_custom_call" | custom-call | flops 14495514624 | bytes 18874368 | tf_op jit(solution)/shard_map/pallas_call | solution.py:347
  183.9 7.1 %add_convert_fusion = bf16[1024,2048]{1,0:T(8,128)(2,1)} fusion(bf16[1024,2048]{1,0:T(8,128)(2,1)} %get-tuple-element.7, bf16[384,1024]{1,0:T(8,128)(2,1)S(1)} %convolution_convert_fusion.1, bf16[384,2048]{1,0:T(8,128)(2,1)} %bitcast.29), kind=kOutput, calls=%fused_computation | convolution fusion | flops 1616904192 | bytes 10747904 | tf_op jit(solution)/shard_map/dot_general | solution.py:417
  (3 shorter events, 0.0 us)
Async XLA Ops:
  0.7 7.7 %collective-permute-start = (s32[2,256]{1,0:T(2,128)S(1)}, s32[2,256]{1,0:T(2,128)S(1)}, u32[]{:S(2)}, u32[]{:S(2)}) collective-permute-start(s32[2,256]{1,0:T(2,128)S(1)} %pad_add_fusion), channel_id=1, source_target_pairs={{4,0},{8,4},{12,8},{16,12},{20,16},{24,20},{28,24},{0,28},{5,1},{9... | collective-permute-start | bytes 6152 | tf_op jit(solution)/shard_map/ppermute | solution.py:17
